TPU v7x, 32 devices: a whole 2x2x4 slice. The times are simulated.
32 devices in a mesh: adapter: 8 (over z, x), tensor: 4 (over y, core).
Axes of the slice: x: 2, y: 2, z: 4, core: 2. Of those that a mesh axis runs over, the one named last changes fastest.
Arguments:
- activations: bfloat16 [4096, 4096], P('adapter', 'tensor'), may hold values from -6 to 6
- output_gradient: bfloat16 [4096, 4096], P('adapter', 'tensor'), may hold values from -6 to 6
- frozen_weight: bfloat16 [4096, 4096], P(None, 'tensor'), may hold values from -0.09375 to 0.09375
- adapter_down_weight: bfloat16 [1024, 4096], P('adapter', 'tensor'), may hold values from -0.09375 to 0.09375
- adapter_up_weight: bfloat16 [1024, 4096], P('adapter', 'tensor'), may hold values from -0.09375 to 0.09375
- adapter_slot_table: int32 [64], replicated, may hold values from 0 to 63, as said below
- group_adapter_index: int32 [8, 6], P('adapter'), may hold values from 0 to 63, as said below
- group_token_length: int32 [8, 6], P('adapter'), may hold values from 1 to 128, as said below
Outputs:
- input_gradient: bfloat16 [4096, 4096], P('adapter', 'tensor')
- down_grad: float32 [1024, 4096], P('adapter', 'tensor')
- up_grad: float32 [1024, 4096], P('adapter', 'tensor')
Inputs may be any that keep to these rules, and one draw needn't show every extreme that they name: `adapter_slot_table`: a permutation of the slots; slot k lies on adapter index k // 8. `group_adapter_index`: the adapters of one index's groups lie on distinct indices of the adapter axis; on every index one group of exactly 128 tokens uses an adapter stored on one index that is the same for all indices. `group_token_length`: each row sums to 512 and holds a group of exactly 128 tokens.
All inputs are finite; a program needn't handle non-finite values.
Results may differ from a plain program's by a relative error of at most 0.015.
Values may be sent and summed in bfloat16 or wider, within the bound.
No kernel may reach another device: no remote copies, remote signals or barrier semaphores. Data moves between devices by JAX's collectives and lax.ppermute only.
A program may use at most 128 MiB of HBM per device.

v0:
```python
import functools

import jax
import jax.numpy as jnp
from jax import lax
from jax.experimental import pallas as pl
from jax.experimental.pallas import tpu as pltpu
from jax.sharding import PartitionSpec as P

RANK = 16
SLOTS = 8
SCALE = 2.0
LANES = 128
VMEM = pl.BlockSpec(memory_space=pltpu.VMEM)
SMEM = pl.BlockSpec(memory_space=pltpu.SMEM)
F32 = jnp.float32
BF16 = jnp.bfloat16
I32 = jnp.int32


def dot(a, b, ca, cb):
    return lax.dot_general(a, b, (((ca,), (cb,)), ((), ())), preferred_element_type=F32)


def exchange(x, axis, k):
    return lax.ppermute(x, axis, [(i, i ^ k) for i in range(lax.axis_size(axis))])


def sds(shape, dtype):
    return jax.ShapeDtypeStruct(shape, dtype)


def call(body, outs, n_vmem, n_smem=0, n_hbm=0, scratch=(), flops=0, moved=0, vmem=16):
    def run(*operands, after=()):
        tokens = len(after)
        at = n_smem + n_vmem + n_hbm

        def wrapped(*refs):
            body(*refs[:at], *refs[at + tokens :])

        return pl.pallas_call(
            wrapped,
            name=getattr(body, "func", body).__name__,
            out_shape=outs,
            in_specs=[SMEM] * n_smem
            + [VMEM] * n_vmem
            + [pl.BlockSpec(memory_space=pltpu.HBM)] * n_hbm
            + [pl.BlockSpec(memory_space=pl.ANY)] * tokens,
            out_specs=jax.tree.map(lambda _: VMEM, outs),
            scratch_shapes=scratch,
            cost_estimate=pl.CostEstimate(flops=flops, bytes_accessed=moved, transcendentals=0),
            compiler_params=pltpu.CompilerParams(vmem_limit_bytes=vmem * 2**20),
        )(*operands, *after)

    return run


def request_body(n, groups, tokens, me_ref, slots_ref, index_ref, length_ref, asked_ref, offset_ref):
    me = me_ref[0]
    lane = lax.broadcasted_iota(I32, (n, LANES), 1)
    row = lax.broadcasted_iota(I32, (n, LANES), 0)
    token = lax.broadcasted_iota(I32, (SLOTS, tokens), 1)
    asked = jnp.zeros((n, LANES), I32)
    offset = jnp.zeros((SLOTS, tokens), I32)
    end = jnp.int32(0)
    for g in range(groups):
        slot = slots_ref[index_ref[0, g]]
        owner = lax.shift_right_logical(slot, 3)
        local = jnp.bitwise_and(slot, SLOTS - 1)
        asked = jnp.where((lane == owner) & (row == me), local + 1, asked)
        offset = jnp.where(token >= end, jnp.bitwise_xor(owner, me), offset)
        end = end + length_ref[0, g]
    asked_ref[...] = asked
    offset_ref[...] = offset


def wanted(me, k, table):
    lane = lax.broadcasted_iota(I32, table.shape, 1)
    row = lax.broadcasted_iota(I32, table.shape, 0)
    mine = jnp.where((lane == me) & (row == jnp.bitwise_xor(me, k)), table, 0)
    return jnp.sum(jnp.sum(mine, axis=1, keepdims=True), axis=0, keepdims=True)


def select_body(ks, me_ref, table_ref, down_ref, up_ref, *out_refs):
    me = me_ref[0]
    table = table_ref[...]
    rows = SLOTS * RANK
    col = lax.broadcasted_iota(I32, (RANK, rows), 1)
    row = lax.broadcasted_iota(I32, (RANK, rows), 0)
    picks = [
        (col == (wanted(me, k, table) - 1) * RANK + row).astype(F32).astype(BF16) for k in ks
    ]
    pick = jnp.concatenate(picks, axis=0)
    up = dot(pick, up_ref[...], 1, 0).astype(BF16)
    down = dot(pick, down_ref[...], 1, 0).astype(BF16)
    for i in range(len(ks)):
        out_refs[i][pl.ds(0, RANK), :] = up[i * RANK : (i + 1) * RANK]
        out_refs[i][pl.ds(RANK, RANK), :] = down[i * RANK : (i + 1) * RANK]


def project_body(ks, offset_ref, x_ref, g_ref, *refs):
    map_refs, out_ref = refs[: len(ks)], refs[len(ks)]
    offset = offset_ref[0:1, :]
    up_maps = jnp.concatenate([m[pl.ds(0, RANK), :] for m in map_refs], axis=0)
    down_maps = jnp.concatenate([m[pl.ds(RANK, RANK), :] for m in map_refs], axis=0)
    up_wide = dot(up_maps, g_ref[...], 1, 1)
    down_wide = dot(down_maps, x_ref[...], 1, 1)
    up = jnp.zeros((RANK, up_wide.shape[1]), F32)
    down = up
    for i, k in enumerate(ks):
        mask = offset == k
        up = up + jnp.where(mask, up_wide[i * RANK : (i + 1) * RANK], 0.0)
        down = down + jnp.where(mask, down_wide[i * RANK : (i + 1) * RANK], 0.0)
    out_ref[pl.ds(0, RANK), :] = up.astype(BF16)
    out_ref[pl.ds(RANK, RANK), :] = down.astype(BF16)


def spread(ks, offset, low):
    zero = jnp.zeros_like(low)
    return jnp.concatenate([jnp.where(offset == k, low, zero) for k in ks], axis=0).astype(BF16)


def gradient_body(ks, parts, offset_ref, x_ref, g_ref, *refs):
    part_refs, out_refs, low_ref = refs[:parts], refs[parts : parts + len(ks)], refs[-1]
    offset = offset_ref[0:1, :]
    total = part_refs[0][...].astype(F32)
    for p in part_refs[1:]:
        total = total + p[...].astype(F32)
    total = total.astype(BF16)
    low_ref[...] = total
    total = total.astype(F32)
    up_wide = spread(ks, offset, total[:RANK])
    down_wide = spread(ks, offset, total[RANK:])
    down_grad = (SCALE * dot(up_wide, x_ref[...], 1, 0)).astype(BF16)
    up_grad = (SCALE * dot(down_wide, g_ref[...], 1, 0)).astype(BF16)
    for i in range(len(ks)):
        out_refs[i][pl.ds(0, RANK), :] = down_grad[i * RANK : (i + 1) * RANK]
        out_refs[i][pl.ds(RANK, RANK), :] = up_grad[i * RANK : (i + 1) * RANK]


def collect_body(ks, me_ref, table_ref, *refs):
    in_refs, down_ref, up_ref = refs[: len(ks)], refs[-2], refs[-1]
    me = me_ref[0]
    table = table_ref[...]
    rows = SLOTS * RANK
    row = lax.broadcasted_iota(I32, (rows, RANK), 0)
    col = lax.broadcasted_iota(I32, (rows, RANK), 1)
    place = jnp.concatenate(
        [(row == (wanted(me, k, table) - 1) * RANK + col).astype(F32).astype(BF16) for k in ks], axis=1
    )
    down = jnp.concatenate([r[pl.ds(0, RANK), :] for r in in_refs], axis=0)
    up = jnp.concatenate([r[pl.ds(RANK, RANK), :] for r in in_refs], axis=0)
    down_ref[...] = dot(place, down, 1, 0)
    up_ref[...] = dot(place, up, 1, 0)


def base_body(tile, loads, adds, at_ref, *refs):
    refs = list(refs)
    if not loads:
        g = refs.pop(0)
    w_ref = refs.pop(0)
    late = refs[: loads + adds]
    out_ref, *inner, held, sems = refs[loads + adds :]
    width = out_ref.shape[1]
    first = at_ref[0] * width
    copies = [
        pltpu.make_async_copy(
            w_ref.at[pl.ds(pl.multiple_of(first + i * tile, tile), tile), :], held.at[i], sems.at[i]
        )
        for i in range(width // tile)
    ]
    others = [
        pltpu.make_async_copy(a, inner[i], sems.at[len(copies) + i]) for i, a in enumerate(late)
    ]
    if loads:
        others[0].start()
        g = inner[0]
    for c in copies:
        c.start()
    for c in others[loads:]:
        c.start()
    if loads:
        others[0].wait()
    for i, c in enumerate(copies):
        c.wait()
        columns = pl.ds(i * tile, tile)
        total = dot(g[...], held[i], 1, 1).astype(BF16)
        if i == 0:
            for o in others[loads:]:
                o.wait()
        for t in inner[loads:]:
            total = (total.astype(F32) + t[:, columns].astype(F32)).astype(BF16)
        out_ref[:, columns] = total


def base_product(gradient, weight, at, width, terms=(), loads=False, after=(), tile=512):
    tokens, depth = gradient.shape
    tiles = width // tile
    late = (gradient,) * loads + terms
    return call(
        functools.partial(base_body, tile, int(loads), len(terms)),
        sds((tokens, width), BF16),
        int(not loads),
        1,
        1 + len(late),
        scratch=[pltpu.VMEM((tokens, depth), BF16)] * len(late)
        + [pltpu.VMEM((tiles, tile, depth), BF16), pltpu.SemaphoreType.DMA((tiles + len(late),))],
        flops=2 * tokens * depth * width,
        moved=2 * depth * width,
        vmem=8,
    )(at, *((gradient,) * (not loads)), weight, *late, after=after)


def finish_body(ks, rows, offset_ref, low_ref, *refs):
    map_refs, term_refs, (out_ref, token_ref) = refs[: len(ks)], refs[len(ks) : -2], refs[-2:]
    down_maps = jnp.concatenate([m[pl.ds(RANK, RANK), :] for m in map_refs], axis=0)
    for first in range(0, out_ref.shape[0], rows):
        at = pl.ds(first, rows)
        up_wide = spread(ks, offset_ref[0:1, at], low_ref[pl.ds(0, RANK), at].astype(F32))
        lora = (SCALE * dot(up_wide, down_maps, 0, 0)).astype(BF16).astype(F32)
        total = term_refs[0][at, :].astype(F32)
        for t in term_refs[1:]:
            total = total + t[at, :].astype(F32)
        out_ref[at, :] = (total + lora).astype(BF16)
    token_ref[...] = jnp.zeros_like(token_ref)


def on_device(x, g, weight, down_maps, up_maps, slot_table, group_index, group_length):
    tokens, width = x.shape
    n = lax.axis_size("adapter")
    tensor = lax.axis_size("tensor")
    groups = group_index.shape[1]
    ks = tuple(range(n - 1, n // 2 - 1, -1)) + (0,) + tuple(range(n // 2 - 1, 0, -1))
    weight, slot_table, group_index, group_length, g_hbm = (
        pltpu.with_memory_space_constraint(a, pltpu.HBM)
        for a in (weight, slot_table, group_index, group_length, g)
    )
    me = lax.axis_index("adapter").astype(I32).reshape(1)
    part = lax.axis_index("tensor").astype(I32)

    asked, offset = call(
        functools.partial(request_body, n, groups, tokens),
        (sds((n, LANES), I32), sds((SLOTS, tokens), I32)),
        0,
        4,
    )(me, slot_table, group_index, group_length)

    def product(k, *after, terms=(), loads=False):
        at = jnp.bitwise_xor(part, k).reshape(1)
        terms = tuple(pltpu.with_memory_space_constraint(t, pltpu.HBM) for t in terms)
        return base_product(g_hbm if loads else g, weight, at, width, terms, loads, after)

    wide = sds((tokens, width), BF16)
    table, tables, hop = asked, [], n // 2
    while hop:
        table = table + exchange(table, "adapter", hop)
        tables.append(table)
        hop //= 2
    far_other = product(3, asked, loads=True)
    far_got = exchange(far_other, "tensor", 1)
    near_other = product(1, far_other, loads=False)
    near_got = exchange(near_other, "tensor", 1)
    far_sum = product(2, tables[0], terms=(far_got,), loads=True)
    across = exchange(far_sum, "tensor", 2)
    sent = call(
        functools.partial(select_body, ks),
        tuple(sds((2 * RANK, width), BF16) for _ in ks),
        3,
        1,
    )(me, table, down_maps, up_maps, after=(far_sum,))
    order = [k for k in ks if k]
    sent = dict(zip(ks, sent))
    got = {k: exchange(sent[k], "adapter", k) for k in order}
    got[0] = sent[0]
    maps = [got[k] for k in ks]
    own_part = call(
        functools.partial(project_body, ks), sds((2 * RANK, tokens), BF16), 3 + n, flops=5000000000
    )(offset, x, g, *maps, after=())
    parts = [own_part] + [exchange(own_part, "tensor", k) for k in range(1, tensor)]
    out = call(
        functools.partial(gradient_body, ks, tensor),
        tuple(sds((2 * RANK, width), BF16) for _ in ks) + (sds((2 * RANK, tokens), BF16),),
        3 + tensor,
        flops=5000000000,
    )(offset, x, g, *parts, after=(across,))
    low = out[-1]
    sums = dict(zip(ks, out))
    got = {k: exchange(sums[k], "adapter", k) for k in order}
    got[0] = sums[0]
    back = [got[k] for k in ks]
    near_sum = product(0, out[-1], terms=(near_got,), loads=False)
    input_gradient, finished = call(
        functools.partial(finish_body, ks, 256), (wide, sds((8, LANES), F32)), 2 + n + 2
    )(offset, low, *maps, near_sum, across)
    down_grad, up_grad = call(
        functools.partial(collect_body, ks),
        (sds((SLOTS * RANK, width), F32), sds((SLOTS * RANK, width), F32)),
        1 + n,
        1,
    )(me, table, *back, after=(finished,))
    return input_gradient, down_grad, up_grad


def solution(mesh):
    in_specs = (
        P("adapter", "tensor"),
        P("adapter", "tensor"),
        P(None, "tensor"),
        P("adapter", "tensor"),
        P("adapter", "tensor"),
        P(),
        P("adapter", None),
        P("adapter", None),
    )
    out_specs = (P("adapter", "tensor"), P("adapter", "tensor"), P("adapter", "tensor"))
    return jax.shard_map(
        on_device, mesh=mesh, in_specs=in_specs, out_specs=out_specs, check_vma=False
    )
```

profile of v0, /device:TPU:0, one launch (start us, length us, event | category | flops | bytes accessed | tf_op | source)
XLA Modules:
  0.0 66.6 jit_solution(4636988178799651203)
XLA Ops:
  0.6 0.7 %request_body.1 = (s32[8,128]{1,0:T(8,128)S(1)}, s32[8,512]{1,0:T(8,128)S(1)}) custom-call(s32[1]{0:T(128)} %bitcast.refs_0_, s32[64]{0:T(128)} %refs_1_.7, s32[1,6]{1,0:T(1,128)} %refs_2_.8, s32[1,6]{1,0:T(1,128)} %refs_3_.2), custom_call_target="tpu_custom_call" | custom-call | tf_op jit(solution)/shard_map/request_body/pallas_call | solution.py:41
  1.3 3.1 %base_body.4.refs_3_ = bf16[512,1024]{1,0:T(8,128)(2,1)S(1)} custom-call(s32[1]{0:T(128)} %bitcast.2.refs_0_, bf16[4096,1024]{1,0:T(8,128)(2,1)} %refs_2_.15, bf16[512,1024]{1,0:T(8,128)(2,1)} %refs_1_.13, s32[8,128]{1,0:T(8,128)S(1)} %get-tuple-element.27.refs_3_), custom_call_target="tpu_custom_call" | custom-call | flops 1073741824 | bytes 2097152 | tf_op jit(solution)/shard_map/base_body/pallas_call | solution.py:41
  4.4 0.0 copy-start.1
  4.4 0.0 copy-start
  4.4 0.5 collective-permute-start.3
  5.0 3.7 %collective-permute-start = (s32[8,128]{1,0:T(8,128)S(1)}, s32[8,128]{1,0:T(8,128)S(1)}, u32[]{:S(2)}, u32[]{:S(2)}) collective-permute-start(s32[8,128]{1,0:T(8,128)S(1)} %get-tuple-element.27.refs_3_), channel_id=1, source_target_pairs={{0,16},{4,20},{8,24},{12,28},{16,0},{20,4},{24,8},{28,12},{1,17},{... | collective-permute-start | bytes 12296 | tf_op jit(solution)/shard_map/ppermute | solution.py:26
  8.6 1.6 %collective-permute-done = s32[8,128]{1,0:T(8,128)S(1)} collective-permute-done((s32[8,128]{1,0:T(8,128)S(1)}, s32[8,128]{1,0:T(8,128)S(1)}, u32[]{:S(2)}, u32[]{:S(2)}) %collective-permute-start) | collective-permute-done | bytes 4128 | tf_op jit(solution)/shard_map/ppermute | solution.py:26
  10.2 0.0 collective-permute-done.3.refs_3_
  10.2 3.2 %base_body.5.refs_4_ = bf16[512,1024]{1,0:T(8,128)(2,1)S(1)} custom-call(s32[1]{0:T(128)} %bitcast.1.refs_0_, bf16[4096,1024]{1,0:T(8,128)(2,1)} %refs_2_.15, bf16[512,1024]{1,0:T(8,128)(2,1)} %refs_1_.13, bf16[512,1024]{1,0:T(8,128)(2,1)} %collective-permute-done.3.refs_3_, s32[8,128]{1,0:T(8,128)S(1)} %add.9.refs_4_), custom_call_target="tpu_custom_call" | custom-call | flops 1073741824 | bytes 2097152 | tf_op jit(solution)/shard_map/base_body/pallas_call | solution.py:41
  13.4 1.9 %collective-permute-start.14 = (bf16[512,1024]{1,0:T(8,128)(2,1)S(1)}, bf16[512,1024]{1,0:T(8,128)(2,1)}, u32[]{:S(2)}, u32[]{:S(2)}) collective-permute-start(bf16[512,1024]{1,0:T(8,128)(2,1)S(1)} %base_body.5.refs_4_), channel_id=1, source_target_pairs={{0,2},{1,3},{2,0},{3,1},{4,6},{5,7},{6,4},{7,5},{8,10},{9,11},{10,... | collective-permute-start | bytes 3145736 | tf_op jit(solution)/shard_map/ppermute | solution.py:26
  15.3 1.6 %collective-permute-start.1 = (s32[8,128]{1,0:T(8,128)S(1)}, s32[8,128]{1,0:T(8,128)S(1)}, u32[]{:S(2)}, u32[]{:S(2)}) collective-permute-start(s32[8,128]{1,0:T(8,128)S(1)} %add.9.refs_4_), channel_id=1, source_target_pairs={{0,8},{4,12},{8,0},{12,4},{16,24},{20,28},{24,16},{28,20},{1,9},{5... | collective-permute-start | bytes 12296 | tf_op jit(solution)/shard_map/ppermute | solution.py:26
  16.9 2.0 %collective-permute-done.1 = s32[8,128]{1,0:T(8,128)S(1)} collective-permute-done((s32[8,128]{1,0:T(8,128)S(1)}, s32[8,128]{1,0:T(8,128)S(1)}, u32[]{:S(2)}, u32[]{:S(2)}) %collective-permute-start.1) | collective-permute-done | bytes 4128 | tf_op jit(solution)/shard_map/ppermute | solution.py:26
  18.9 1.5 %collective-permute-start.2 = (s32[8,128]{1,0:T(8,128)S(1)}, s32[8,128]{1,0:T(8,128)S(1)}, u32[]{:S(2)}, u32[]{:S(2)}) collective-permute-start(s32[8,128]{1,0:T(8,128)S(1)} %add.10), channel_id=1, source_target_pairs={{0,4},{4,0},{8,12},{12,8},{16,20},{20,16},{24,28},{28,24},{1,5},{5... | collective-permute-start | bytes 12296 | tf_op jit(solution)/shard_map/ppermute | solution.py:26
  20.4 2.1 %collective-permute-done.2 = s32[8,128]{1,0:T(8,128)S(1)} collective-permute-done((s32[8,128]{1,0:T(8,128)S(1)}, s32[8,128]{1,0:T(8,128)S(1)}, u32[]{:S(2)}, u32[]{:S(2)}) %collective-permute-start.2) | collective-permute-done | bytes 4128 | tf_op jit(solution)/shard_map/ppermute | solution.py:26
  22.6 0.9 %copy-done.2 = bf16[128,1024]{1,0:T(8,128)(2,1)S(1)} copy-done((bf16[128,1024]{1,0:T(8,128)(2,1)S(1)}, bf16[128,1024]{1,0:T(8,128)(2,1)}, u32[]{:S(2)}) %copy-start.2) | copy-done | bytes 262168
  23.5 1.0 %select_body.1 = (bf16[32,1024]{1,0:T(8,128)(2,1)}, bf16[32,1024]{1,0:T(8,128)(2,1)}, bf16[32,1024]{1,0:T(8,128)(2,1)}, bf16[32,1024]{1,0:T(8,128)(2,1)S(1)}, bf...) custom-call(s32[1]{0:T(128)} %bitcast.refs_0_, ...), custom_call_target="tpu_custom_call" | custom-call | tf_op jit(solution)/shard_map/select_body/pallas_call | solution.py:41
  24.5 4.6 %collective-permute-start.4 = (bf16[32,1024]{1,0:T(8,128)(2,1)}, bf16[32,1024]{1,0:T(8,128)(2,1)S(1)}, u32[]{:S(2)}, u32[]{:S(2)}) collective-permute-start(bf16[32,1024]{1,0:T(8,128)(2,1)} %get-tuple-element.28), channel_id=1, source_target_pairs={{0,28},{4,24},{8,20},{12,16},{16,12},{20,8},{24,4},{28,0},{1,29},{... | collective-permute-start | bytes 196616 | tf_op jit(solution)/shard_map/ppermute | solution.py:26
  29.1 0.2 collective-permute-start.5
  29.4 0.8 %collective-permute-start.6 = (bf16[32,1024]{1,0:T(8,128)(2,1)}, bf16[32,1024]{1,0:T(8,128)(2,1)S(1)}, u32[]{:S(2)}, u32[]{:S(2)}) collective-permute-start(bf16[32,1024]{1,0:T(8,128)(2,1)} %get-tuple-element.30), channel_id=1, source_target_pairs={{0,20},{4,16},{8,28},{12,24},{16,4},{20,0},{24,12},{28,8},{1,21},{... | collective-permute-start | bytes 196616 | tf_op jit(solution)/shard_map/ppermute | solution.py:26
  30.2 2.1 %collective-permute-start.7 = (bf16[32,1024]{1,0:T(8,128)(2,1)}, bf16[32,1024]{1,0:T(8,128)(2,1)S(1)}, u32[]{:S(2)}, u32[]{:S(2)}) collective-permute-start(bf16[32,1024]{1,0:T(8,128)(2,1)} %copy-done.7), channel_id=1, source_target_pairs={{0,16},{4,20},{8,24},{12,28},{16,0},{20,4},{24,8},{28,12},{1,17},{... | collective-permute-start | bytes 196616 | tf_op jit(solution)/shard_map/ppermute | solution.py:26
  32.3 0.2 collective-permute-done.4.refs_3_.refs_2_
  32.5 3.4 %collective-permute-start.8 = (bf16[32,1024]{1,0:T(8,128)(2,1)}, bf16[32,1024]{1,0:T(8,128)(2,1)S(1)}, u32[]{:S(2)}, u32[]{:S(2)}) collective-permute-start(bf16[32,1024]{1,0:T(8,128)(2,1)} %copy-done.6), channel_id=1, source_target_pairs={{0,12},{4,8},{8,4},{12,0},{16,28},{20,24},{24,20},{28,16},{1,13},{... | collective-permute-start | bytes 196616 | tf_op jit(solution)/shard_map/ppermute | solution.py:26
  35.9 0.0 collective-permute-done.5.refs_4_.refs_3_
  35.9 1.5 %collective-permute-start.9 = (bf16[32,1024]{1,0:T(8,128)(2,1)}, bf16[32,1024]{1,0:T(8,128)(2,1)S(1)}, u32[]{:S(2)}, u32[]{:S(2)}) collective-permute-start(bf16[32,1024]{1,0:T(8,128)(2,1)} %copy-done.5), channel_id=1, source_target_pairs={{0,8},{4,12},{8,0},{12,4},{16,24},{20,28},{24,16},{28,20},{1,9},{5... | collective-permute-start | bytes 196616 | tf_op jit(solution)/shard_map/ppermute | solution.py:26
  37.4 0.6 collective-permute-done.6.refs_5_.refs_4_
  38.0 1.1 %collective-permute-start.10 = (bf16[32,1024]{1,0:T(8,128)(2,1)}, bf16[32,1024]{1,0:T(8,128)(2,1)S(1)}, u32[]{:S(2)}, u32[]{:S(2)}) collective-permute-start(bf16[32,1024]{1,0:T(8,128)(2,1)} %copy-done.4), channel_id=1, source_target_pairs={{0,4},{4,0},{8,12},{12,8},{16,20},{20,16},{24,28},{28,24},{1,5},{5... | collective-permute-start | bytes 196616 | tf_op jit(solution)/shard_map/ppermute | solution.py:26
  39.1 2.7 %base_body.6 = bf16[512,1024]{1,0:T(8,128)(2,1)S(1)} custom-call(s32[1]{0:T(128)} %bitcast.4.refs_0_, bf16[512,1024]{1,0:T(8,128)(2,1)S(1)} %copy-done, bf16[4096,1024]{1,0:T(8,128)(2,1)} %refs_2_.15, bf16[512,1024]{1,0:T(8,128)(2,1)S(1)} %base_body.4.refs_3_), custom_call_target="tpu_custom_call" | custom-call | flops 1073741824 | bytes 2097152 | tf_op jit(solution)/shard_map/base_body/pallas_call | solution.py:41
  41.9 0.0 collective-permute-done.7.refs_6_.refs_5_
  41.9 0.1 collective-permute-start.15
  42.0 0.0 collective-permute-done.8.refs_8_.refs_7_
  42.0 0.0 collective-permute-done.9.refs_9_.refs_8_
  42.0 0.5 collective-permute-done.10.refs_10_.refs_9_
  42.5 0.8 %project_body.1.refs_3_ = bf16[32,512]{1,0:T(8,128)(2,1)S(1)} custom-call(s32[8,512]{1,0:T(8,128)S(1)} %get-tuple-element.26.refs_0_, bf16[512,1024]{1,0:T(8,128)(2,1)S(1)} %copy-done.3, bf16[512,1024]{1,0:T(8,128)(2,1)S(1)} %copy-done, bf16[32,1024]{1,0:T(8,128)(2,1)S(1)} %collective-permute-done.4.refs_3_.refs_2_, ...), custom_call_target="tpu_custom_call" | custom-call | flops 5000000000 | tf_op jit(solution)/shard_map/project_body/pallas_call | solution.py:41
  43.3 0.2 collective-permute-start.13
  43.5 1.5 %collective-permute-start.12 = (bf16[32,512]{1,0:T(8,128)(2,1)S(1)}, bf16[32,512]{1,0:T(8,128)(2,1)S(1)}, u32[]{:S(2)}, u32[]{:S(2)}) collective-permute-start(bf16[32,512]{1,0:T(8,128)(2,1)S(1)} %project_body.1.refs_3_), channel_id=1, source_target_pairs={{0,2},{1,3},{2,0},{3,1},{4,6},{5,7},{6,4},{7,5},{8,10},{9,11},{10,... | collective-permute-start | bytes 98312 | tf_op jit(solution)/shard_map/ppermute | solution.py:26
  45.0 0.2 collective-permute-start.11
  45.2 1.6 %collective-permute-done.13.refs_6_ = bf16[32,512]{1,0:T(8,128)(2,1)S(1)} collective-permute-done((bf16[32,512]{1,0:T(8,128)(2,1)S(1)}, bf16[32,512]{1,0:T(8,128)(2,1)S(1)}, u32[]{:S(2)}, u32[]{:S(2)}) %collective-permute-start.13) | collective-permute-done | bytes 32800 | tf_op jit(solution)/shard_map/ppermute | solution.py:26
  46.9 0.9 %collective-permute-done.12.refs_5_ = bf16[32,512]{1,0:T(8,128)(2,1)S(1)} collective-permute-done((bf16[32,512]{1,0:T(8,128)(2,1)S(1)}, bf16[32,512]{1,0:T(8,128)(2,1)S(1)}, u32[]{:S(2)}, u32[]{:S(2)}) %collective-permute-start.12) | collective-permute-done | bytes 32800 | tf_op jit(solution)/shard_map/ppermute | solution.py:26
  47.8 0.5 gradient_body.1
  48.2 2.7 %collective-permute-start.16 = (bf16[32,1024]{1,0:T(8,128)(2,1)S(1)}, bf16[32,1024]{1,0:T(8,128)(2,1)S(1)}, u32[]{:S(2)}, u32[]{:S(2)}) collective-permute-start(bf16[32,1024]{1,0:T(8,128)(2,1)S(1)} %get-tuple-element.38), channel_id=1, source_target_pairs={{0,28},{4,24},{8,20},{12,16},{16,12},{20,8},{24,4},{28,0},{1,29},{... | collective-permute-start | bytes 196616 | tf_op jit(solution)/shard_map/ppermute | solution.py:26
  50.9 1.7 %collective-permute-start.17 = (bf16[32,1024]{1,0:T(8,128)(2,1)S(1)}, bf16[32,1024]{1,0:T(8,128)(2,1)S(1)}, u32[]{:S(2)}, u32[]{:S(2)}) collective-permute-start(bf16[32,1024]{1,0:T(8,128)(2,1)S(1)} %get-tuple-element.39), channel_id=1, source_target_pairs={{0,24},{4,28},{8,16},{12,20},{16,8},{20,12},{24,0},{28,4},{1,25},{... | collective-permute-start | bytes 196616 | tf_op jit(solution)/shard_map/ppermute | solution.py:26
  52.6 3.4 %collective-permute-start.19 = (bf16[32,1024]{1,0:T(8,128)(2,1)S(1)}, bf16[32,1024]{1,0:T(8,128)(2,1)S(1)}, u32[]{:S(2)}, u32[]{:S(2)}) collective-permute-start(bf16[32,1024]{1,0:T(8,128)(2,1)S(1)} %get-tuple-element.41), channel_id=1, source_target_pairs={{0,16},{4,20},{8,24},{12,28},{16,0},{20,4},{24,8},{28,12},{1,17},{... | collective-permute-start | bytes 196616 | tf_op jit(solution)/shard_map/ppermute | solution.py:26
  56.0 0.3 collective-permute-start.20
  56.3 2.2 %collective-permute-start.21 = (bf16[32,1024]{1,0:T(8,128)(2,1)S(1)}, bf16[32,1024]{1,0:T(8,128)(2,1)S(1)}, u32[]{:S(2)}, u32[]{:S(2)}) collective-permute-start(bf16[32,1024]{1,0:T(8,128)(2,1)S(1)} %get-tuple-element.44), channel_id=1, source_target_pairs={{0,8},{4,12},{8,0},{12,4},{16,24},{20,28},{24,16},{28,20},{1,9},{5... | collective-permute-start | bytes 196616 | tf_op jit(solution)/shard_map/ppermute | solution.py:26
  58.5 1.0 %collective-permute-start.22 = (bf16[32,1024]{1,0:T(8,128)(2,1)S(1)}, bf16[32,1024]{1,0:T(8,128)(2,1)S(1)}, u32[]{:S(2)}, u32[]{:S(2)}) collective-permute-start(bf16[32,1024]{1,0:T(8,128)(2,1)S(1)} %get-tuple-element.45), channel_id=1, source_target_pairs={{0,4},{4,0},{8,12},{12,8},{16,20},{20,16},{24,28},{28,24},{1,5},{5... | collective-permute-start | bytes 196616 | tf_op jit(solution)/shard_map/ppermute | solution.py:26
  59.5 2.9 %base_body.7.refs_10_ = bf16[512,1024]{1,0:T(8,128)(2,1)S(1)} custom-call(s32[1]{0:T(128)} %bitcast.3.refs_0_, bf16[512,1024]{1,0:T(8,128)(2,1)S(1)} %copy-done, bf16[4096,1024]{1,0:T(8,128)(2,1)} %refs_2_.15, bf16[512,1024]{1,0:T(8,128)(2,1)} %copy-done.8, bf16[32,512]{1,0:T(8,128)(2,1)S(1)} %get-tuple-element.36.refs_4_.refs_1_), custom_call_target="tpu_custom_call" | custom-call | flops 1073741824 | bytes 2097152 | tf_op jit(solution)/shard_map/base_body/pallas_call | solution.py:41
  62.3 2.8 %finish_body.1 = (bf16[512,1024]{1,0:T(8,128)(2,1)}, f32[8,128]{1,0:T(8,128)S(1)}) custom-call(s32[8,512]{1,0:T(8,128)S(1)} %get-tuple-element.26.refs_0_, bf16[32,512]{1,0:T(8,128)(2,1)S(1)} %get-tuple-element.36.refs_4_.refs_1_, bf16[32,1024]{1,0:T(8,128)(2,1)S(1)} %collective-permute-done.4.refs_3_.refs_2_, ...), custom_call_target="tpu_custom_call" | custom-call | tf_op jit(solution)/shard_map/finish_body/pallas_call | solution.py:41
  65.2 1.4 %collect_body.1 = (f32[128,1024]{1,0:T(8,128)}, f32[128,1024]{1,0:T(8,128)}) custom-call(s32[1]{0:T(128)} %bitcast.refs_0_, s32[8,128]{1,0:T(8,128)S(1)} %add.11.refs_1_, bf16[32,1024]{1,0:T(8,128)(2,1)S(1)} %collective-permute-done.16.refs_2_, bf16[32,1024]{1,0:T(8,128)(2,1)S(1)} %collective-permute-done.17.refs_3_, ...), custom_call_target="tpu_custom_call" | custom-call | tf_op jit(solution)/shard_map/collect_body/pallas_call | solution.py:41
  (29 shorter events, 0.1 us)
Async XLA Ops:
  4.4 18.1 %copy-start.1 = (bf16[128,1024]{1,0:T(8,128)(2,1)S(1)}, bf16[128,1024]{1,0:T(8,128)(2,1)}, u32[]{:S(2)}) copy-start(bf16[128,1024]{1,0:T(8,128)(2,1)} %refs_2_.11) | copy-start | bytes 786436
  4.4 34.7 %copy-start = (bf16[512,1024]{1,0:T(8,128)(2,1)S(1)}, bf16[512,1024]{1,0:T(8,128)(2,1)}, u32[]{:S(2)}) copy-start(bf16[512,1024]{1,0:T(8,128)(2,1)} %refs_1_.13) | copy-start | bytes 3145732
  4.4 5.8 %collective-permute-start.3 = (bf16[512,1024]{1,0:T(8,128)(2,1)S(1)}, bf16[512,1024]{1,0:T(8,128)(2,1)}, u32[]{:S(2)}, u32[]{:S(2)}) collective-permute-start(bf16[512,1024]{1,0:T(8,128)(2,1)S(1)} %base_body.4.refs_3_), channel_id=1, source_target_pairs={{0,1},{1,0},{2,3},{3,2},{4,5},{5,4},{6,7},{7,6},{8,9},{9,8},{10,11... | collective-permute-start | bytes 3145736 | tf_op jit(solution)/shard_map/ppermute | solution.py:26
  5.0 5.3 %collective-permute-start = (s32[8,128]{1,0:T(8,128)S(1)}, s32[8,128]{1,0:T(8,128)S(1)}, u32[]{:S(2)}, u32[]{:S(2)}) collective-permute-start(s32[8,128]{1,0:T(8,128)S(1)} %get-tuple-element.27.refs_3_), channel_id=1, source_target_pairs={{0,16},{4,20},{8,24},{12,28},{16,0},{20,4},{24,8},{28,12},{1,17},{... | collective-permute-start | bytes 12296 | tf_op jit(solution)/shard_map/ppermute | solution.py:26
  13.4 34.4 %collective-permute-start.14 = (bf16[512,1024]{1,0:T(8,128)(2,1)S(1)}, bf16[512,1024]{1,0:T(8,128)(2,1)}, u32[]{:S(2)}, u32[]{:S(2)}) collective-permute-start(bf16[512,1024]{1,0:T(8,128)(2,1)S(1)} %base_body.5.refs_4_), channel_id=1, source_target_pairs={{0,2},{1,3},{2,0},{3,1},{4,6},{5,7},{6,4},{7,5},{8,10},{9,11},{10,... | collective-permute-start | bytes 3145736 | tf_op jit(solution)/shard_map/ppermute | solution.py:26
  15.3 3.6 %collective-permute-start.1 = (s32[8,128]{1,0:T(8,128)S(1)}, s32[8,128]{1,0:T(8,128)S(1)}, u32[]{:S(2)}, u32[]{:S(2)}) collective-permute-start(s32[8,128]{1,0:T(8,128)S(1)} %add.9.refs_4_), channel_id=1, source_target_pairs={{0,8},{4,12},{8,0},{12,4},{16,24},{20,28},{24,16},{28,20},{1,9},{5... | collective-permute-start | bytes 12296 | tf_op jit(solution)/shard_map/ppermute | solution.py:26
  18.9 3.6 %collective-permute-start.2 = (s32[8,128]{1,0:T(8,128)S(1)}, s32[8,128]{1,0:T(8,128)S(1)}, u32[]{:S(2)}, u32[]{:S(2)}) collective-permute-start(s32[8,128]{1,0:T(8,128)S(1)} %add.10), channel_id=1, source_target_pairs={{0,4},{4,0},{8,12},{12,8},{16,20},{20,16},{24,28},{28,24},{1,5},{5... | collective-permute-start | bytes 12296 | tf_op jit(solution)/shard_map/ppermute | solution.py:26
  22.6 1.0 %copy-start.2 = (bf16[128,1024]{1,0:T(8,128)(2,1)S(1)}, bf16[128,1024]{1,0:T(8,128)(2,1)}, u32[]{:S(2)}) copy-start(bf16[128,1024]{1,0:T(8,128)(2,1)} %refs_3_.3) | copy-start | bytes 786436
  24.5 4.8 %copy-start.4 = (bf16[32,1024]{1,0:T(8,128)(2,1)}, bf16[32,1024]{1,0:T(8,128)(2,1)S(1)}, u32[]{:S(2)}) copy-start(bf16[32,1024]{1,0:T(8,128)(2,1)S(1)} %get-tuple-element.35) | copy-start | bytes 196612
  24.5 4.8 %copy-start.5 = (bf16[32,1024]{1,0:T(8,128)(2,1)}, bf16[32,1024]{1,0:T(8,128)(2,1)S(1)}, u32[]{:S(2)}) copy-start(bf16[32,1024]{1,0:T(8,128)(2,1)S(1)} %get-tuple-element.34) | copy-start | bytes 196612
  24.5 4.8 %copy-start.6 = (bf16[32,1024]{1,0:T(8,128)(2,1)}, bf16[32,1024]{1,0:T(8,128)(2,1)S(1)}, u32[]{:S(2)}) copy-start(bf16[32,1024]{1,0:T(8,128)(2,1)S(1)} %get-tuple-element.33) | copy-start | bytes 196612
  24.5 4.8 %copy-start.7 = (bf16[32,1024]{1,0:T(8,128)(2,1)}, bf16[32,1024]{1,0:T(8,128)(2,1)S(1)}, u32[]{:S(2)}) copy-start(bf16[32,1024]{1,0:T(8,128)(2,1)S(1)} %get-tuple-element.31) | copy-start | bytes 196612
  24.5 8.0 %collective-permute-start.4 = (bf16[32,1024]{1,0:T(8,128)(2,1)}, bf16[32,1024]{1,0:T(8,128)(2,1)S(1)}, u32[]{:S(2)}, u32[]{:S(2)}) collective-permute-start(bf16[32,1024]{1,0:T(8,128)(2,1)} %get-tuple-element.28), channel_id=1, source_target_pairs={{0,28},{4,24},{8,20},{12,16},{16,12},{20,8},{24,4},{28,0},{1,29},{... | collective-permute-start | bytes 196616 | tf_op jit(solution)/shard_map/ppermute | solution.py:26
  29.1 6.8 %collective-permute-start.5 = (bf16[32,1024]{1,0:T(8,128)(2,1)}, bf16[32,1024]{1,0:T(8,128)(2,1)S(1)}, u32[]{:S(2)}, u32[]{:S(2)}) collective-permute-start(bf16[32,1024]{1,0:T(8,128)(2,1)} %get-tuple-element.29), channel_id=1, source_target_pairs={{0,24},{4,28},{8,16},{12,20},{16,8},{20,12},{24,0},{28,4},{1,25},{... | collective-permute-start | bytes 196616 | tf_op jit(solution)/shard_map/ppermute | solution.py:26
  29.4 8.7 %collective-permute-start.6 = (bf16[32,1024]{1,0:T(8,128)(2,1)}, bf16[32,1024]{1,0:T(8,128)(2,1)S(1)}, u32[]{:S(2)}, u32[]{:S(2)}) collective-permute-start(bf16[32,1024]{1,0:T(8,128)(2,1)} %get-tuple-element.30), channel_id=1, source_target_pairs={{0,20},{4,16},{8,28},{12,24},{16,4},{20,0},{24,12},{28,8},{1,21},{... | collective-permute-start | bytes 196616 | tf_op jit(solution)/shard_map/ppermute | solution.py:26
  30.2 12.3 %copy-start.3 = (bf16[512,1024]{1,0:T(8,128)(2,1)S(1)}, bf16[512,1024]{1,0:T(8,128)(2,1)}, u32[]{:S(2)}) copy-start(bf16[512,1024]{1,0:T(8,128)(2,1)} %refs_1_.11) | copy-start | bytes 3145732
  30.2 11.7 %collective-permute-start.7 = (bf16[32,1024]{1,0:T(8,128)(2,1)}, bf16[32,1024]{1,0:T(8,128)(2,1)S(1)}, u32[]{:S(2)}, u32[]{:S(2)}) collective-permute-start(bf16[32,1024]{1,0:T(8,128)(2,1)} %copy-done.7), channel_id=1, source_target_pairs={{0,16},{4,20},{8,24},{12,28},{16,0},{20,4},{24,8},{28,12},{1,17},{... | collective-permute-start | bytes 196616 | tf_op jit(solution)/shard_map/ppermute | solution.py:26
  32.5 9.5 %collective-permute-start.8 = (bf16[32,1024]{1,0:T(8,128)(2,1)}, bf16[32,1024]{1,0:T(8,128)(2,1)S(1)}, u32[]{:S(2)}, u32[]{:S(2)}) collective-permute-start(bf16[32,1024]{1,0:T(8,128)(2,1)} %copy-done.6), channel_id=1, source_target_pairs={{0,12},{4,8},{8,4},{12,0},{16,28},{20,24},{24,20},{28,16},{1,13},{... | collective-permute-start | bytes 196616 | tf_op jit(solution)/shard_map/ppermute | solution.py:26
  35.9 6.1 %collective-permute-start.9 = (bf16[32,1024]{1,0:T(8,128)(2,1)}, bf16[32,1024]{1,0:T(8,128)(2,1)S(1)}, u32[]{:S(2)}, u32[]{:S(2)}) collective-permute-start(bf16[32,1024]{1,0:T(8,128)(2,1)} %copy-done.5), channel_id=1, source_target_pairs={{0,8},{4,12},{8,0},{12,4},{16,24},{20,28},{24,16},{28,20},{1,9},{5... | collective-permute-start | bytes 196616 | tf_op jit(solution)/shard_map/ppermute | solution.py:26
  38.0 4.5 %collective-permute-start.10 = (bf16[32,1024]{1,0:T(8,128)(2,1)}, bf16[32,1024]{1,0:T(8,128)(2,1)S(1)}, u32[]{:S(2)}, u32[]{:S(2)}) collective-permute-start(bf16[32,1024]{1,0:T(8,128)(2,1)} %copy-done.4), channel_id=1, source_target_pairs={{0,4},{4,0},{8,12},{12,8},{16,20},{20,16},{24,28},{28,24},{1,5},{5... | collective-permute-start | bytes 196616 | tf_op jit(solution)/shard_map/ppermute | solution.py:26
  41.9 14.1 %collective-permute-start.15 = (bf16[512,1024]{1,0:T(8,128)(2,1)S(1)}, bf16[512,1024]{1,0:T(8,128)(2,1)S(1)}, u32[]{:S(2)}, u32[]{:S(2)}) collective-permute-start(bf16[512,1024]{1,0:T(8,128)(2,1)S(1)} %base_body.6), channel_id=1, source_target_pairs={{0,1},{1,0},{2,3},{3,2},{4,5},{5,4},{6,7},{7,6},{8,9},{9,8},{10,11... | collective-permute-start | bytes 3145736 | tf_op jit(solution)/shard_map/ppermute | solution.py:26
  43.3 3.6 %collective-permute-start.13 = (bf16[32,512]{1,0:T(8,128)(2,1)S(1)}, bf16[32,512]{1,0:T(8,128)(2,1)S(1)}, u32[]{:S(2)}, u32[]{:S(2)}) collective-permute-start(bf16[32,512]{1,0:T(8,128)(2,1)S(1)} %project_body.1.refs_3_), channel_id=1, source_target_pairs={{0,3},{1,2},{2,1},{3,0},{4,7},{5,6},{6,5},{7,4},{8,11},{9,10},{10,... | collective-permute-start | bytes 98312 | tf_op jit(solution)/shard_map/ppermute | solution.py:26
  43.5 4.3 %collective-permute-start.12 = (bf16[32,512]{1,0:T(8,128)(2,1)S(1)}, bf16[32,512]{1,0:T(8,128)(2,1)S(1)}, u32[]{:S(2)}, u32[]{:S(2)}) collective-permute-start(bf16[32,512]{1,0:T(8,128)(2,1)S(1)} %project_body.1.refs_3_), channel_id=1, source_target_pairs={{0,2},{1,3},{2,0},{3,1},{4,6},{5,7},{6,4},{7,5},{8,10},{9,11},{10,... | collective-permute-start | bytes 98312 | tf_op jit(solution)/shard_map/ppermute | solution.py:26
  45.0 2.8 %collective-permute-start.11 = (bf16[32,512]{1,0:T(8,128)(2,1)S(1)}, bf16[32,512]{1,0:T(8,128)(2,1)S(1)}, u32[]{:S(2)}, u32[]{:S(2)}) collective-permute-start(bf16[32,512]{1,0:T(8,128)(2,1)S(1)} %project_body.1.refs_3_), channel_id=1, source_target_pairs={{0,1},{1,0},{2,3},{3,2},{4,5},{5,4},{6,7},{7,6},{8,9},{9,8},{10,11... | collective-permute-start | bytes 98312 | tf_op jit(solution)/shard_map/ppermute | solution.py:26
  48.2 8.0 %collective-permute-start.16 = (bf16[32,1024]{1,0:T(8,128)(2,1)S(1)}, bf16[32,1024]{1,0:T(8,128)(2,1)S(1)}, u32[]{:S(2)}, u32[]{:S(2)}) collective-permute-start(bf16[32,1024]{1,0:T(8,128)(2,1)S(1)} %get-tuple-element.38), channel_id=1, source_target_pairs={{0,28},{4,24},{8,20},{12,16},{16,12},{20,8},{24,4},{28,0},{1,29},{... | collective-permute-start | bytes 196616 | tf_op jit(solution)/shard_map/ppermute | solution.py:26
  50.9 7.5 %collective-permute-start.17 = (bf16[32,1024]{1,0:T(8,128)(2,1)S(1)}, bf16[32,1024]{1,0:T(8,128)(2,1)S(1)}, u32[]{:S(2)}, u32[]{:S(2)}) collective-permute-start(bf16[32,1024]{1,0:T(8,128)(2,1)S(1)} %get-tuple-element.39), channel_id=1, source_target_pairs={{0,24},{4,28},{8,16},{12,20},{16,8},{20,12},{24,0},{28,4},{1,25},{... | collective-permute-start | bytes 196616 | tf_op jit(solution)/shard_map/ppermute | solution.py:26
  52.6 12.6 %collective-permute-start.18 = (bf16[32,1024]{1,0:T(8,128)(2,1)S(1)}, bf16[32,1024]{1,0:T(8,128)(2,1)S(1)}, u32[]{:S(2)}, u32[]{:S(2)}) collective-permute-start(bf16[32,1024]{1,0:T(8,128)(2,1)S(1)} %get-tuple-element.40), channel_id=1, source_target_pairs={{0,20},{4,16},{8,28},{12,24},{16,4},{20,0},{24,12},{28,8},{1,21},{... | collective-permute-start | bytes 196616 | tf_op jit(solution)/shard_map/ppermute | solution.py:26
  52.6 12.6 %collective-permute-start.19 = (bf16[32,1024]{1,0:T(8,128)(2,1)S(1)}, bf16[32,1024]{1,0:T(8,128)(2,1)S(1)}, u32[]{:S(2)}, u32[]{:S(2)}) collective-permute-start(bf16[32,1024]{1,0:T(8,128)(2,1)S(1)} %get-tuple-element.41), channel_id=1, source_target_pairs={{0,16},{4,20},{8,24},{12,28},{16,0},{20,4},{24,8},{28,12},{1,17},{... | collective-permute-start | bytes 196616 | tf_op jit(solution)/shard_map/ppermute | solution.py:26
  56.0 3.5 %copy-start.8 = (bf16[512,1024]{1,0:T(8,128)(2,1)}, bf16[512,1024]{1,0:T(8,128)(2,1)S(1)}, u32[]{:S(2)}) copy-start(bf16[512,1024]{1,0:T(8,128)(2,1)S(1)} %collective-permute-done.15.refs_3_) | copy-start | bytes 3145732
  56.0 9.2 %collective-permute-start.20 = (bf16[32,1024]{1,0:T(8,128)(2,1)S(1)}, bf16[32,1024]{1,0:T(8,128)(2,1)S(1)}, u32[]{:S(2)}, u32[]{:S(2)}) collective-permute-start(bf16[32,1024]{1,0:T(8,128)(2,1)S(1)} %get-tuple-element.43), channel_id=1, source_target_pairs={{0,12},{4,8},{8,4},{12,0},{16,28},{20,24},{24,20},{28,16},{1,13},{... | collective-permute-start | bytes 196616 | tf_op jit(solution)/shard_map/ppermute | solution.py:26
  56.3 8.9 %collective-permute-start.21 = (bf16[32,1024]{1,0:T(8,128)(2,1)S(1)}, bf16[32,1024]{1,0:T(8,128)(2,1)S(1)}, u32[]{:S(2)}, u32[]{:S(2)}) collective-permute-start(bf16[32,1024]{1,0:T(8,128)(2,1)S(1)} %get-tuple-element.44), channel_id=1, source_target_pairs={{0,8},{4,12},{8,0},{12,4},{16,24},{20,28},{24,16},{28,20},{1,9},{5... | collective-permute-start | bytes 196616 | tf_op jit(solution)/shard_map/ppermute | solution.py:26
  58.5 6.7 %collective-permute-start.22 = (bf16[32,1024]{1,0:T(8,128)(2,1)S(1)}, bf16[32,1024]{1,0:T(8,128)(2,1)S(1)}, u32[]{:S(2)}, u32[]{:S(2)}) collective-permute-start(bf16[32,1024]{1,0:T(8,128)(2,1)S(1)} %get-tuple-element.45), channel_id=1, source_target_pairs={{0,4},{4,0},{8,12},{12,8},{16,20},{20,16},{24,28},{28,24},{1,5},{5... | collective-permute-start | bytes 196616 | tf_op jit(solution)/shard_map/ppermute | solution.py:26
where the time goes:
time: 66.8 us; the launch traced here: 66.6 us
  starting transfers between devices  36.2 us (54%)
  Pallas kernels  19 us (28%)
  waiting for transfers between devices  9.59 us (14%)
  local copies, waits for them, and re-layouts  0.98 us (1%)
  between operations  0.8 us (1%)
    ppermute x23, starting transfers between devices, exchange(): lax.ppermute(x, axis, [(i, i ^ k) for i in range(lax.axis_size(axis))])  36.2 us
    pallas_call x10, Pallas kernels, run(): pl.pallas_call(wrapped, name=getattr(body, 'func', body).__name__, out_sh...  19 us
    ppermute x23, waiting for transfers between devices, exchange(): lax.ppermute(x, axis, [(i, i ^ k) for i in range(lax.axis_size(axis))])  9.59 us
  transfers between devices with their start and end apart: 23, of which 8 were waited for; matrix products, arithmetic and copies ran while one was open for 0% of the time, Pallas kernels for 16%

commit v1 on v0

--- a/solution.py
+++ b/solution.py
@@ -211,17 +211,36 @@
     )(at, *((gradient,) * (not loads)), weight, *late, after=after)
 
 
-def finish_body(ks, rows, offset_ref, low_ref, *refs):
-    map_refs, term_refs, (out_ref, token_ref) = refs[: len(ks)], refs[len(ks) : -2], refs[-2:]
+def finish_body(ks, tile, at_ref, offset_ref, low_ref, *refs):
+    map_refs, refs = refs[: len(ks)], refs[len(ks) :]
+    g_ref, w_ref, near_ref, far_ref, out_ref, token_ref, near, far, held, sems = refs
+    depth, width = held.shape[2], out_ref.shape[1]
+    tiles = width // tile
+    first = at_ref[0] * width
+    copies = [
+        pltpu.make_async_copy(
+            w_ref.at[pl.ds(pl.multiple_of(first + i * tile, tile), tile), :], held.at[i], sems.at[i]
+        )
+        for i in range(tiles)
+    ]
+    terms = [
+        pltpu.make_async_copy(near_ref, near, sems.at[tiles]),
+        pltpu.make_async_copy(far_ref, far, sems.at[tiles + 1]),
+    ]
+    for c in copies + terms:
+        c.start()
     down_maps = jnp.concatenate([m[pl.ds(RANK, RANK), :] for m in map_refs], axis=0)
-    for first in range(0, out_ref.shape[0], rows):
-        at = pl.ds(first, rows)
-        up_wide = spread(ks, offset_ref[0:1, at], low_ref[pl.ds(0, RANK), at].astype(F32))
-        lora = (SCALE * dot(up_wide, down_maps, 0, 0)).astype(BF16).astype(F32)
-        total = term_refs[0][at, :].astype(F32)
-        for t in term_refs[1:]:
-            total = total + t[at, :].astype(F32)
-        out_ref[at, :] = (total + lora).astype(BF16)
+    up_wide = spread(ks, offset_ref[0:1, :], low_ref[pl.ds(0, RANK), :].astype(F32))
+    for i, c in enumerate(copies):
+        c.wait()
+        at = slice(i * tile, (i + 1) * tile)
+        total = dot(g_ref[...], held[i], 1, 1).astype(BF16).astype(F32)
+        if i == 0:
+            for t in terms:
+                t.wait()
+        total = total + near[:, at].astype(F32) + far[:, at].astype(F32)
+        lora = (SCALE * dot(up_wide, down_maps[:, at], 0, 0)).astype(BF16).astype(F32)
+        out_ref[:, at] = (total + lora).astype(BF16)
     token_ref[...] = jnp.zeros_like(token_ref)
 
 
@@ -288,10 +307,18 @@
     got = {k: exchange(sums[k], "adapter", k) for k in order}
     got[0] = sums[0]
     back = [got[k] for k in ks]
-    near_sum = product(0, out[-1], terms=(near_got,), loads=False)
+    near_got, across = (pltpu.with_memory_space_constraint(a, pltpu.HBM) for a in (near_got, across))
+    tile = width // 2
     input_gradient, finished = call(
-        functools.partial(finish_body, ks, 256), (wide, sds((8, LANES), F32)), 2 + n + 2
-    )(offset, low, *maps, near_sum, across)
+        functools.partial(finish_body, ks, tile),
+        (wide, sds((8, LANES), F32)),
+        2 + n + 1,
+        1,
+        3,
+        scratch=[pltpu.VMEM((tokens, width), BF16)] * 2
+        + [pltpu.VMEM((2, tile, width), BF16), pltpu.SemaphoreType.DMA((4,))],
+        flops=2 * tokens * width * width,
+    )(part.reshape(1), offset, low, *maps, g, weight, near_got, across)
     down_grad, up_grad = call(
         functools.partial(collect_body, ks),
         (sds((SLOTS * RANK, width), F32), sds((SLOTS * RANK, width), F32)),

time: 66.8 us -> 65.6 us (0.982)
  Pallas kernels: 19 us -> 17.9 us
    pallas_call x10 -> x9, Pallas kernels: 19 us -> 17.9 us  [run(): pl.pallas_call(wrapped, name=getattr(body, 'func', body).__name__, out_sh...]
  transfers between devices with their start and end apart: 23 -> 23, of which waited for: 8 -> 8; matrix products, arithmetic and copies ran while one was open for 0% -> 0% of each run, Pallas kernels for 16% -> 15%
where the time goes in v1:
time: 65.6 us; the launch traced here: 65.5 us
  starting transfers between devices  36.2 us (55%)
  Pallas kernels  17.9 us (27%)
  waiting for transfers between devices  9.59 us (15%)
  local copies, waits for them, and re-layouts  0.98 us (1%)
  between operations  0.82 us (1%)
    ppermute x23, starting transfers between devices, exchange(): lax.ppermute(x, axis, [(i, i ^ k) for i in range(lax.axis_size(axis))])  36.2 us
    pallas_call x9, Pallas kernels, run(): pl.pallas_call(wrapped, name=getattr(body, 'func', body).__name__, out_sh...  17.9 us
    ppermute x23, waiting for transfers between devices, exchange(): lax.ppermute(x, axis, [(i, i ^ k) for i in range(lax.axis_size(axis))])  9.59 us
  transfers between devices with their start and end apart: 23, of which 8 were waited for; matrix products, arithmetic and copies ran while one was open for 0% of the time, Pallas kernels for 15%

profile of v1, /device:TPU:0, one launch (start us, length us, event | category | flops | bytes accessed | tf_op | source)
XLA Modules:
  0.0 65.5 jit_solution(10094147524387461263)
XLA Ops:
  0.6 0.7 %request_body.1 = (s32[8,128]{1,0:T(8,128)S(1)}, s32[8,512]{1,0:T(8,128)S(1)}) custom-call(s32[1]{0:T(128)} %bitcast.1.refs_0_, s32[64]{0:T(128)} %refs_1_.6, s32[1,6]{1,0:T(1,128)} %refs_2_.7, s32[1,6]{1,0:T(1,128)} %refs_3_.2), custom_call_target="tpu_custom_call" | custom-call | tf_op jit(solution)/shard_map/request_body/pallas_call | solution.py:41
  1.3 3.1 %base_body.3.refs_3_ = bf16[512,1024]{1,0:T(8,128)(2,1)S(1)} custom-call(s32[1]{0:T(128)} %bitcast.3.refs_0_, bf16[4096,1024]{1,0:T(8,128)(2,1)} %refs_12_.1, bf16[512,1024]{1,0:T(8,128)(2,1)} %refs_11_.1, s32[8,128]{1,0:T(8,128)S(1)} %get-tuple-element.27.refs_3_), custom_call_target="tpu_custom_call" | custom-call | flops 1073741824 | bytes 2097152 | tf_op jit(solution)/shard_map/base_body/pallas_call | solution.py:41
  4.4 0.0 copy-start.1
  4.4 0.0 copy-start
  4.4 0.5 collective-permute-start.3
  5.0 3.7 %collective-permute-start = (s32[8,128]{1,0:T(8,128)S(1)}, s32[8,128]{1,0:T(8,128)S(1)}, u32[]{:S(2)}, u32[]{:S(2)}) collective-permute-start(s32[8,128]{1,0:T(8,128)S(1)} %get-tuple-element.27.refs_3_), channel_id=1, source_target_pairs={{0,16},{4,20},{8,24},{12,28},{16,0},{20,4},{24,8},{28,12},{1,17},{... | collective-permute-start | bytes 12296 | tf_op jit(solution)/shard_map/ppermute | solution.py:26
  8.6 1.6 %collective-permute-done = s32[8,128]{1,0:T(8,128)S(1)} collective-permute-done((s32[8,128]{1,0:T(8,128)S(1)}, s32[8,128]{1,0:T(8,128)S(1)}, u32[]{:S(2)}, u32[]{:S(2)}) %collective-permute-start) | collective-permute-done | bytes 4128 | tf_op jit(solution)/shard_map/ppermute | solution.py:26
  10.2 0.0 collective-permute-done.3.refs_3_
  10.2 3.2 %base_body.4.refs_4_ = bf16[512,1024]{1,0:T(8,128)(2,1)S(1)} custom-call(s32[1]{0:T(128)} %bitcast.2.refs_0_, bf16[4096,1024]{1,0:T(8,128)(2,1)} %refs_12_.1, bf16[512,1024]{1,0:T(8,128)(2,1)} %refs_11_.1, bf16[512,1024]{1,0:T(8,128)(2,1)} %collective-permute-done.3.refs_3_, s32[8,128]{1,0:T(8,128)S(1)} %add.9.refs_4_), custom_call_target="tpu_custom_call" | custom-call | flops 1073741824 | bytes 2097152 | tf_op jit(solution)/shard_map/base_body/pallas_call | solution.py:41
  13.4 1.9 %collective-permute-start.14 = (bf16[512,1024]{1,0:T(8,128)(2,1)S(1)}, bf16[512,1024]{1,0:T(8,128)(2,1)}, u32[]{:S(2)}, u32[]{:S(2)}) collective-permute-start(bf16[512,1024]{1,0:T(8,128)(2,1)S(1)} %base_body.4.refs_4_), channel_id=1, source_target_pairs={{0,2},{1,3},{2,0},{3,1},{4,6},{5,7},{6,4},{7,5},{8,10},{9,11},{10,... | collective-permute-start | bytes 3145736 | tf_op jit(solution)/shard_map/ppermute | solution.py:26
  15.3 1.6 %collective-permute-start.1 = (s32[8,128]{1,0:T(8,128)S(1)}, s32[8,128]{1,0:T(8,128)S(1)}, u32[]{:S(2)}, u32[]{:S(2)}) collective-permute-start(s32[8,128]{1,0:T(8,128)S(1)} %add.9.refs_4_), channel_id=1, source_target_pairs={{0,8},{4,12},{8,0},{12,4},{16,24},{20,28},{24,16},{28,20},{1,9},{5... | collective-permute-start | bytes 12296 | tf_op jit(solution)/shard_map/ppermute | solution.py:26
  16.9 2.0 %collective-permute-done.1 = s32[8,128]{1,0:T(8,128)S(1)} collective-permute-done((s32[8,128]{1,0:T(8,128)S(1)}, s32[8,128]{1,0:T(8,128)S(1)}, u32[]{:S(2)}, u32[]{:S(2)}) %collective-permute-start.1) | collective-permute-done | bytes 4128 | tf_op jit(solution)/shard_map/ppermute | solution.py:26
  18.9 1.5 %collective-permute-start.2 = (s32[8,128]{1,0:T(8,128)S(1)}, s32[8,128]{1,0:T(8,128)S(1)}, u32[]{:S(2)}, u32[]{:S(2)}) collective-permute-start(s32[8,128]{1,0:T(8,128)S(1)} %add.10), channel_id=1, source_target_pairs={{0,4},{4,0},{8,12},{12,8},{16,20},{20,16},{24,28},{28,24},{1,5},{5... | collective-permute-start | bytes 12296 | tf_op jit(solution)/shard_map/ppermute | solution.py:26
  20.4 2.1 %collective-permute-done.2 = s32[8,128]{1,0:T(8,128)S(1)} collective-permute-done((s32[8,128]{1,0:T(8,128)S(1)}, s32[8,128]{1,0:T(8,128)S(1)}, u32[]{:S(2)}, u32[]{:S(2)}) %collective-permute-start.2) | collective-permute-done | bytes 4128 | tf_op jit(solution)/shard_map/ppermute | solution.py:26
  22.6 0.9 %copy-done.2 = bf16[128,1024]{1,0:T(8,128)(2,1)S(1)} copy-done((bf16[128,1024]{1,0:T(8,128)(2,1)S(1)}, bf16[128,1024]{1,0:T(8,128)(2,1)}, u32[]{:S(2)}) %copy-start.2) | copy-done | bytes 262168
  23.5 1.0 %select_body.1 = (bf16[32,1024]{1,0:T(8,128)(2,1)}, bf16[32,1024]{1,0:T(8,128)(2,1)}, bf16[32,1024]{1,0:T(8,128)(2,1)}, bf16[32,1024]{1,0:T(8,128)(2,1)S(1)}, bf...) custom-call(s32[1]{0:T(128)} %bitcast.1.refs_0_, ...), custom_call_target="tpu_custom_call" | custom-call | tf_op jit(solution)/shard_map/select_body/pallas_call | solution.py:41
  24.5 4.6 %collective-permute-start.4 = (bf16[32,1024]{1,0:T(8,128)(2,1)}, bf16[32,1024]{1,0:T(8,128)(2,1)S(1)}, u32[]{:S(2)}, u32[]{:S(2)}) collective-permute-start(bf16[32,1024]{1,0:T(8,128)(2,1)} %get-tuple-element.28), channel_id=1, source_target_pairs={{0,28},{4,24},{8,20},{12,16},{16,12},{20,8},{24,4},{28,0},{1,29},{... | collective-permute-start | bytes 196616 | tf_op jit(solution)/shard_map/ppermute | solution.py:26
  29.1 0.2 collective-permute-start.5
  29.4 0.8 %collective-permute-start.6 = (bf16[32,1024]{1,0:T(8,128)(2,1)}, bf16[32,1024]{1,0:T(8,128)(2,1)S(1)}, u32[]{:S(2)}, u32[]{:S(2)}) collective-permute-start(bf16[32,1024]{1,0:T(8,128)(2,1)} %get-tuple-element.30), channel_id=1, source_target_pairs={{0,20},{4,16},{8,28},{12,24},{16,4},{20,0},{24,12},{28,8},{1,21},{... | collective-permute-start | bytes 196616 | tf_op jit(solution)/shard_map/ppermute | solution.py:26
  30.2 2.1 %collective-permute-start.7 = (bf16[32,1024]{1,0:T(8,128)(2,1)}, bf16[32,1024]{1,0:T(8,128)(2,1)S(1)}, u32[]{:S(2)}, u32[]{:S(2)}) collective-permute-start(bf16[32,1024]{1,0:T(8,128)(2,1)} %copy-done.7), channel_id=1, source_target_pairs={{0,16},{4,20},{8,24},{12,28},{16,0},{20,4},{24,8},{28,12},{1,17},{... | collective-permute-start | bytes 196616 | tf_op jit(solution)/shard_map/ppermute | solution.py:26
  32.3 0.2 collective-permute-done.4.refs_3_
  32.5 3.4 %collective-permute-start.8 = (bf16[32,1024]{1,0:T(8,128)(2,1)}, bf16[32,1024]{1,0:T(8,128)(2,1)S(1)}, u32[]{:S(2)}, u32[]{:S(2)}) collective-permute-start(bf16[32,1024]{1,0:T(8,128)(2,1)} %copy-done.6), channel_id=1, source_target_pairs={{0,12},{4,8},{8,4},{12,0},{16,28},{20,24},{24,20},{28,16},{1,13},{... | collective-permute-start | bytes 196616 | tf_op jit(solution)/shard_map/ppermute | solution.py:26
  35.9 0.0 collective-permute-done.5.refs_4_
  35.9 1.5 %collective-permute-start.9 = (bf16[32,1024]{1,0:T(8,128)(2,1)}, bf16[32,1024]{1,0:T(8,128)(2,1)S(1)}, u32[]{:S(2)}, u32[]{:S(2)}) collective-permute-start(bf16[32,1024]{1,0:T(8,128)(2,1)} %copy-done.5), channel_id=1, source_target_pairs={{0,8},{4,12},{8,0},{12,4},{16,24},{20,28},{24,16},{28,20},{1,9},{5... | collective-permute-start | bytes 196616 | tf_op jit(solution)/shard_map/ppermute | solution.py:26
  37.4 0.6 collective-permute-done.6.refs_5_
  38.0 1.1 %collective-permute-start.10 = (bf16[32,1024]{1,0:T(8,128)(2,1)}, bf16[32,1024]{1,0:T(8,128)(2,1)S(1)}, u32[]{:S(2)}, u32[]{:S(2)}) collective-permute-start(bf16[32,1024]{1,0:T(8,128)(2,1)} %copy-done.4), channel_id=1, source_target_pairs={{0,4},{4,0},{8,12},{12,8},{16,20},{20,16},{24,28},{28,24},{1,5},{5... | collective-permute-start | bytes 196616 | tf_op jit(solution)/shard_map/ppermute | solution.py:26
  39.1 2.7 %base_body.5 = bf16[512,1024]{1,0:T(8,128)(2,1)S(1)} custom-call(s32[1]{0:T(128)} %bitcast.4.refs_0_, bf16[512,1024]{1,0:T(8,128)(2,1)S(1)} %copy-done, bf16[4096,1024]{1,0:T(8,128)(2,1)} %refs_12_.1, bf16[512,1024]{1,0:T(8,128)(2,1)S(1)} %base_body.3.refs_3_), custom_call_target="tpu_custom_call" | custom-call | flops 1073741824 | bytes 2097152 | tf_op jit(solution)/shard_map/base_body/pallas_call | solution.py:41
  41.9 0.0 collective-permute-done.7.refs_6_
  41.9 0.1 collective-permute-start.15
  42.0 0.0 collective-permute-done.8.refs_8_
  42.0 0.0 collective-permute-done.9.refs_9_
  42.0 0.5 collective-permute-done.10.refs_10_
  42.5 0.8 %project_body.1.refs_3_ = bf16[32,512]{1,0:T(8,128)(2,1)S(1)} custom-call(s32[8,512]{1,0:T(8,128)S(1)} %get-tuple-element.26.refs_0_.refs_1_, bf16[512,1024]{1,0:T(8,128)(2,1)S(1)} %copy-done.3, bf16[512,1024]{1,0:T(8,128)(2,1)S(1)} %copy-done, bf16[32,1024]{1,0:T(8,128)(2,1)S(1)} %collective-permute-done.4.refs_3_, ...), custom_call_target="tpu_custom_call" | custom-call | flops 5000000000 | tf_op jit(solution)/shard_map/project_body/pallas_call | solution.py:41
  43.3 0.2 collective-permute-start.13
  43.5 1.5 %collective-permute-start.12 = (bf16[32,512]{1,0:T(8,128)(2,1)S(1)}, bf16[32,512]{1,0:T(8,128)(2,1)S(1)}, u32[]{:S(2)}, u32[]{:S(2)}) collective-permute-start(bf16[32,512]{1,0:T(8,128)(2,1)S(1)} %project_body.1.refs_3_), channel_id=1, source_target_pairs={{0,2},{1,3},{2,0},{3,1},{4,6},{5,7},{6,4},{7,5},{8,10},{9,11},{10,... | collective-permute-start | bytes 98312 | tf_op jit(solution)/shard_map/ppermute | solution.py:26
  45.0 0.2 collective-permute-start.11
  45.2 1.6 %collective-permute-done.13.refs_6_ = bf16[32,512]{1,0:T(8,128)(2,1)S(1)} collective-permute-done((bf16[32,512]{1,0:T(8,128)(2,1)S(1)}, bf16[32,512]{1,0:T(8,128)(2,1)S(1)}, u32[]{:S(2)}, u32[]{:S(2)}) %collective-permute-start.13) | collective-permute-done | bytes 32800 | tf_op jit(solution)/shard_map/ppermute | solution.py:26
  46.9 0.9 %collective-permute-done.12.refs_5_ = bf16[32,512]{1,0:T(8,128)(2,1)S(1)} collective-permute-done((bf16[32,512]{1,0:T(8,128)(2,1)S(1)}, bf16[32,512]{1,0:T(8,128)(2,1)S(1)}, u32[]{:S(2)}, u32[]{:S(2)}) %collective-permute-start.12) | collective-permute-done | bytes 32800 | tf_op jit(solution)/shard_map/ppermute | solution.py:26
  47.8 0.5 gradient_body.1
  48.2 2.7 %collective-permute-start.16 = (bf16[32,1024]{1,0:T(8,128)(2,1)S(1)}, bf16[32,1024]{1,0:T(8,128)(2,1)S(1)}, u32[]{:S(2)}, u32[]{:S(2)}) collective-permute-start(bf16[32,1024]{1,0:T(8,128)(2,1)S(1)} %get-tuple-element.38), channel_id=1, source_target_pairs={{0,28},{4,24},{8,20},{12,16},{16,12},{20,8},{24,4},{28,0},{1,29},{... | collective-permute-start | bytes 196616 | tf_op jit(solution)/shard_map/ppermute | solution.py:26
  50.9 1.7 %collective-permute-start.17 = (bf16[32,1024]{1,0:T(8,128)(2,1)S(1)}, bf16[32,1024]{1,0:T(8,128)(2,1)S(1)}, u32[]{:S(2)}, u32[]{:S(2)}) collective-permute-start(bf16[32,1024]{1,0:T(8,128)(2,1)S(1)} %get-tuple-element.39), channel_id=1, source_target_pairs={{0,24},{4,28},{8,16},{12,20},{16,8},{20,12},{24,0},{28,4},{1,25},{... | collective-permute-start | bytes 196616 | tf_op jit(solution)/shard_map/ppermute | solution.py:26
  52.6 0.0 collective-permute-start.18
  52.6 3.4 %collective-permute-start.19 = (bf16[32,1024]{1,0:T(8,128)(2,1)S(1)}, bf16[32,1024]{1,0:T(8,128)(2,1)S(1)}, u32[]{:S(2)}, u32[]{:S(2)}) collective-permute-start(bf16[32,1024]{1,0:T(8,128)(2,1)S(1)} %get-tuple-element.41), channel_id=1, source_target_pairs={{0,16},{4,20},{8,24},{12,28},{16,0},{20,4},{24,8},{28,12},{1,17},{... | collective-permute-start | bytes 196616 | tf_op jit(solution)/shard_map/ppermute | solution.py:26
  56.0 0.3 collective-permute-start.20
  56.3 2.2 %collective-permute-start.21 = (bf16[32,1024]{1,0:T(8,128)(2,1)S(1)}, bf16[32,1024]{1,0:T(8,128)(2,1)S(1)}, u32[]{:S(2)}, u32[]{:S(2)}) collective-permute-start(bf16[32,1024]{1,0:T(8,128)(2,1)S(1)} %get-tuple-element.44), channel_id=1, source_target_pairs={{0,8},{4,12},{8,0},{12,4},{16,24},{20,28},{24,16},{28,20},{1,9},{5... | collective-permute-start | bytes 196616 | tf_op jit(solution)/shard_map/ppermute | solution.py:26
  58.5 1.0 %collective-permute-start.22 = (bf16[32,1024]{1,0:T(8,128)(2,1)S(1)}, bf16[32,1024]{1,0:T(8,128)(2,1)S(1)}, u32[]{:S(2)}, u32[]{:S(2)}) collective-permute-start(bf16[32,1024]{1,0:T(8,128)(2,1)S(1)} %get-tuple-element.45), channel_id=1, source_target_pairs={{0,4},{4,0},{8,12},{12,8},{16,20},{20,16},{24,28},{28,24},{1,5},{5... | collective-permute-start | bytes 196616 | tf_op jit(solution)/shard_map/ppermute | solution.py:26
  59.5 4.6 %finish_body.1 = (bf16[512,1024]{1,0:T(8,128)(2,1)}, f32[8,128]{1,0:T(8,128)S(1)}) custom-call(s32[1]{0:T(128)} %bitcast.refs_0_, s32[8,512]{1,0:T(8,128)S(1)} %get-tuple-element.26.refs_0_.refs_1_, bf16[32,512]{1,0:T(8,128)(2,1)S(1)} %get-tuple-element.36.refs_2_, bf16[32,1024]{1,0:T(8,128)(2,1)S(1)} %collective-permute-done.4.refs_3_, ...), custom_call_target="tpu_custom_call" | custom-call | flops 1073741824 | tf_op jit(solution)/shard_map/finish_body/pallas_call | solution.py:41
  64.1 1.4 %collect_body.1 = (f32[128,1024]{1,0:T(8,128)}, f32[128,1024]{1,0:T(8,128)}) custom-call(s32[1]{0:T(128)} %bitcast.1.refs_0_, s32[8,128]{1,0:T(8,128)S(1)} %add.11.refs_1_, bf16[32,1024]{1,0:T(8,128)(2,1)S(1)} %collective-permute-done.16.refs_2_, bf16[32,1024]{1,0:T(8,128)(2,1)S(1)} %collective-permute-done.17.refs_3_, ...), custom_call_target="tpu_custom_call" | custom-call | tf_op jit(solution)/shard_map/collect_body/pallas_call | solution.py:41
  (28 shorter events, 0.1 us)
Async XLA Ops:
  4.4 18.1 %copy-start.1 = (bf16[128,1024]{1,0:T(8,128)(2,1)S(1)}, bf16[128,1024]{1,0:T(8,128)(2,1)}, u32[]{:S(2)}) copy-start(bf16[128,1024]{1,0:T(8,128)(2,1)} %refs_2_.10) | copy-start | bytes 786436
  4.4 34.7 %copy-start = (bf16[512,1024]{1,0:T(8,128)(2,1)S(1)}, bf16[512,1024]{1,0:T(8,128)(2,1)}, u32[]{:S(2)}) copy-start(bf16[512,1024]{1,0:T(8,128)(2,1)} %refs_11_.1) | copy-start | bytes 3145732
  4.4 5.8 %collective-permute-start.3 = (bf16[512,1024]{1,0:T(8,128)(2,1)S(1)}, bf16[512,1024]{1,0:T(8,128)(2,1)}, u32[]{:S(2)}, u32[]{:S(2)}) collective-permute-start(bf16[512,1024]{1,0:T(8,128)(2,1)S(1)} %base_body.3.refs_3_), channel_id=1, source_target_pairs={{0,1},{1,0},{2,3},{3,2},{4,5},{5,4},{6,7},{7,6},{8,9},{9,8},{10,11... | collective-permute-start | bytes 3145736 | tf_op jit(solution)/shard_map/ppermute | solution.py:26
  5.0 5.3 %collective-permute-start = (s32[8,128]{1,0:T(8,128)S(1)}, s32[8,128]{1,0:T(8,128)S(1)}, u32[]{:S(2)}, u32[]{:S(2)}) collective-permute-start(s32[8,128]{1,0:T(8,128)S(1)} %get-tuple-element.27.refs_3_), channel_id=1, source_target_pairs={{0,16},{4,20},{8,24},{12,28},{16,0},{20,4},{24,8},{28,12},{1,17},{... | collective-permute-start | bytes 12296 | tf_op jit(solution)/shard_map/ppermute | solution.py:26
  13.4 34.4 %collective-permute-start.14 = (bf16[512,1024]{1,0:T(8,128)(2,1)S(1)}, bf16[512,1024]{1,0:T(8,128)(2,1)}, u32[]{:S(2)}, u32[]{:S(2)}) collective-permute-start(bf16[512,1024]{1,0:T(8,128)(2,1)S(1)} %base_body.4.refs_4_), channel_id=1, source_target_pairs={{0,2},{1,3},{2,0},{3,1},{4,6},{5,7},{6,4},{7,5},{8,10},{9,11},{10,... | collective-permute-start | bytes 3145736 | tf_op jit(solution)/shard_map/ppermute | solution.py:26
  15.3 3.6 %collective-permute-start.1 = (s32[8,128]{1,0:T(8,128)S(1)}, s32[8,128]{1,0:T(8,128)S(1)}, u32[]{:S(2)}, u32[]{:S(2)}) collective-permute-start(s32[8,128]{1,0:T(8,128)S(1)} %add.9.refs_4_), channel_id=1, source_target_pairs={{0,8},{4,12},{8,0},{12,4},{16,24},{20,28},{24,16},{28,20},{1,9},{5... | collective-permute-start | bytes 12296 | tf_op jit(solution)/shard_map/ppermute | solution.py:26
  18.9 3.6 %collective-permute-start.2 = (s32[8,128]{1,0:T(8,128)S(1)}, s32[8,128]{1,0:T(8,128)S(1)}, u32[]{:S(2)}, u32[]{:S(2)}) collective-permute-start(s32[8,128]{1,0:T(8,128)S(1)} %add.10), channel_id=1, source_target_pairs={{0,4},{4,0},{8,12},{12,8},{16,20},{20,16},{24,28},{28,24},{1,5},{5... | collective-permute-start | bytes 12296 | tf_op jit(solution)/shard_map/ppermute | solution.py:26
  22.6 1.0 %copy-start.2 = (bf16[128,1024]{1,0:T(8,128)(2,1)S(1)}, bf16[128,1024]{1,0:T(8,128)(2,1)}, u32[]{:S(2)}) copy-start(bf16[128,1024]{1,0:T(8,128)(2,1)} %refs_3_.3) | copy-start | bytes 786436
  24.5 4.8 %copy-start.4 = (bf16[32,1024]{1,0:T(8,128)(2,1)}, bf16[32,1024]{1,0:T(8,128)(2,1)S(1)}, u32[]{:S(2)}) copy-start(bf16[32,1024]{1,0:T(8,128)(2,1)S(1)} %get-tuple-element.35) | copy-start | bytes 196612
  24.5 4.8 %copy-start.5 = (bf16[32,1024]{1,0:T(8,128)(2,1)}, bf16[32,1024]{1,0:T(8,128)(2,1)S(1)}, u32[]{:S(2)}) copy-start(bf16[32,1024]{1,0:T(8,128)(2,1)S(1)} %get-tuple-element.34) | copy-start | bytes 196612
  24.5 4.8 %copy-start.6 = (bf16[32,1024]{1,0:T(8,128)(2,1)}, bf16[32,1024]{1,0:T(8,128)(2,1)S(1)}, u32[]{:S(2)}) copy-start(bf16[32,1024]{1,0:T(8,128)(2,1)S(1)} %get-tuple-element.33) | copy-start | bytes 196612
  24.5 4.8 %copy-start.7 = (bf16[32,1024]{1,0:T(8,128)(2,1)}, bf16[32,1024]{1,0:T(8,128)(2,1)S(1)}, u32[]{:S(2)}) copy-start(bf16[32,1024]{1,0:T(8,128)(2,1)S(1)} %get-tuple-element.31) | copy-start | bytes 196612
  24.5 8.0 %collective-permute-start.4 = (bf16[32,1024]{1,0:T(8,128)(2,1)}, bf16[32,1024]{1,0:T(8,128)(2,1)S(1)}, u32[]{:S(2)}, u32[]{:S(2)}) collective-permute-start(bf16[32,1024]{1,0:T(8,128)(2,1)} %get-tuple-element.28), channel_id=1, source_target_pairs={{0,28},{4,24},{8,20},{12,16},{16,12},{20,8},{24,4},{28,0},{1,29},{... | collective-permute-start | bytes 196616 | tf_op jit(solution)/shard_map/ppermute | solution.py:26
  29.1 6.8 %collective-permute-start.5 = (bf16[32,1024]{1,0:T(8,128)(2,1)}, bf16[32,1024]{1,0:T(8,128)(2,1)S(1)}, u32[]{:S(2)}, u32[]{:S(2)}) collective-permute-start(bf16[32,1024]{1,0:T(8,128)(2,1)} %get-tuple-element.29), channel_id=1, source_target_pairs={{0,24},{4,28},{8,16},{12,20},{16,8},{20,12},{24,0},{28,4},{1,25},{... | collective-permute-start | bytes 196616 | tf_op jit(solution)/shard_map/ppermute | solution.py:26
  29.4 8.7 %collective-permute-start.6 = (bf16[32,1024]{1,0:T(8,128)(2,1)}, bf16[32,1024]{1,0:T(8,128)(2,1)S(1)}, u32[]{:S(2)}, u32[]{:S(2)}) collective-permute-start(bf16[32,1024]{1,0:T(8,128)(2,1)} %get-tuple-element.30), channel_id=1, source_target_pairs={{0,20},{4,16},{8,28},{12,24},{16,4},{20,0},{24,12},{28,8},{1,21},{... | collective-permute-start | bytes 196616 | tf_op jit(solution)/shard_map/ppermute | solution.py:26
  30.2 12.3 %copy-start.3 = (bf16[512,1024]{1,0:T(8,128)(2,1)S(1)}, bf16[512,1024]{1,0:T(8,128)(2,1)}, u32[]{:S(2)}) copy-start(bf16[512,1024]{1,0:T(8,128)(2,1)} %refs_1_.10) | copy-start | bytes 3145732
  30.2 11.7 %collective-permute-start.7 = (bf16[32,1024]{1,0:T(8,128)(2,1)}, bf16[32,1024]{1,0:T(8,128)(2,1)S(1)}, u32[]{:S(2)}, u32[]{:S(2)}) collective-permute-start(bf16[32,1024]{1,0:T(8,128)(2,1)} %copy-done.7), channel_id=1, source_target_pairs={{0,16},{4,20},{8,24},{12,28},{16,0},{20,4},{24,8},{28,12},{1,17},{... | collective-permute-start | bytes 196616 | tf_op jit(solution)/shard_map/ppermute | solution.py:26
  32.5 9.5 %collective-permute-start.8 = (bf16[32,1024]{1,0:T(8,128)(2,1)}, bf16[32,1024]{1,0:T(8,128)(2,1)S(1)}, u32[]{:S(2)}, u32[]{:S(2)}) collective-permute-start(bf16[32,1024]{1,0:T(8,128)(2,1)} %copy-done.6), channel_id=1, source_target_pairs={{0,12},{4,8},{8,4},{12,0},{16,28},{20,24},{24,20},{28,16},{1,13},{... | collective-permute-start | bytes 196616 | tf_op jit(solution)/shard_map/ppermute | solution.py:26
  35.9 6.1 %collective-permute-start.9 = (bf16[32,1024]{1,0:T(8,128)(2,1)}, bf16[32,1024]{1,0:T(8,128)(2,1)S(1)}, u32[]{:S(2)}, u32[]{:S(2)}) collective-permute-start(bf16[32,1024]{1,0:T(8,128)(2,1)} %copy-done.5), channel_id=1, source_target_pairs={{0,8},{4,12},{8,0},{12,4},{16,24},{20,28},{24,16},{28,20},{1,9},{5... | collective-permute-start | bytes 196616 | tf_op jit(solution)/shard_map/ppermute | solution.py:26
  38.0 4.5 %collective-permute-start.10 = (bf16[32,1024]{1,0:T(8,128)(2,1)}, bf16[32,1024]{1,0:T(8,128)(2,1)S(1)}, u32[]{:S(2)}, u32[]{:S(2)}) collective-permute-start(bf16[32,1024]{1,0:T(8,128)(2,1)} %copy-done.4), channel_id=1, source_target_pairs={{0,4},{4,0},{8,12},{12,8},{16,20},{20,16},{24,28},{28,24},{1,5},{5... | collective-permute-start | bytes 196616 | tf_op jit(solution)/shard_map/ppermute | solution.py:26
  41.9 14.1 %collective-permute-start.15 = (bf16[512,1024]{1,0:T(8,128)(2,1)S(1)}, bf16[512,1024]{1,0:T(8,128)(2,1)S(1)}, u32[]{:S(2)}, u32[]{:S(2)}) collective-permute-start(bf16[512,1024]{1,0:T(8,128)(2,1)S(1)} %base_body.5), channel_id=1, source_target_pairs={{0,1},{1,0},{2,3},{3,2},{4,5},{5,4},{6,7},{7,6},{8,9},{9,8},{10,11... | collective-permute-start | bytes 3145736 | tf_op jit(solution)/shard_map/ppermute | solution.py:26
  43.3 3.6 %collective-permute-start.13 = (bf16[32,512]{1,0:T(8,128)(2,1)S(1)}, bf16[32,512]{1,0:T(8,128)(2,1)S(1)}, u32[]{:S(2)}, u32[]{:S(2)}) collective-permute-start(bf16[32,512]{1,0:T(8,128)(2,1)S(1)} %project_body.1.refs_3_), channel_id=1, source_target_pairs={{0,3},{1,2},{2,1},{3,0},{4,7},{5,6},{6,5},{7,4},{8,11},{9,10},{10,... | collective-permute-start | bytes 98312 | tf_op jit(solution)/shard_map/ppermute | solution.py:26
  43.5 4.3 %collective-permute-start.12 = (bf16[32,512]{1,0:T(8,128)(2,1)S(1)}, bf16[32,512]{1,0:T(8,128)(2,1)S(1)}, u32[]{:S(2)}, u32[]{:S(2)}) collective-permute-start(bf16[32,512]{1,0:T(8,128)(2,1)S(1)} %project_body.1.refs_3_), channel_id=1, source_target_pairs={{0,2},{1,3},{2,0},{3,1},{4,6},{5,7},{6,4},{7,5},{8,10},{9,11},{10,... | collective-permute-start | bytes 98312 | tf_op jit(solution)/shard_map/ppermute | solution.py:26
  45.0 2.8 %collective-permute-start.11 = (bf16[32,512]{1,0:T(8,128)(2,1)S(1)}, bf16[32,512]{1,0:T(8,128)(2,1)S(1)}, u32[]{:S(2)}, u32[]{:S(2)}) collective-permute-start(bf16[32,512]{1,0:T(8,128)(2,1)S(1)} %project_body.1.refs_3_), channel_id=1, source_target_pairs={{0,1},{1,0},{2,3},{3,2},{4,5},{5,4},{6,7},{7,6},{8,9},{9,8},{10,11... | collective-permute-start | bytes 98312 | tf_op jit(solution)/shard_map/ppermute | solution.py:26
  48.2 8.0 %collective-permute-start.16 = (bf16[32,1024]{1,0:T(8,128)(2,1)S(1)}, bf16[32,1024]{1,0:T(8,128)(2,1)S(1)}, u32[]{:S(2)}, u32[]{:S(2)}) collective-permute-start(bf16[32,1024]{1,0:T(8,128)(2,1)S(1)} %get-tuple-element.38), channel_id=1, source_target_pairs={{0,28},{4,24},{8,20},{12,16},{16,12},{20,8},{24,4},{28,0},{1,29},{... | collective-permute-start | bytes 196616 | tf_op jit(solution)/shard_map/ppermute | solution.py:26
  50.9 7.5 %collective-permute-start.17 = (bf16[32,1024]{1,0:T(8,128)(2,1)S(1)}, bf16[32,1024]{1,0:T(8,128)(2,1)S(1)}, u32[]{:S(2)}, u32[]{:S(2)}) collective-permute-start(bf16[32,1024]{1,0:T(8,128)(2,1)S(1)} %get-tuple-element.39), channel_id=1, source_target_pairs={{0,24},{4,28},{8,16},{12,20},{16,8},{20,12},{24,0},{28,4},{1,25},{... | collective-permute-start | bytes 196616 | tf_op jit(solution)/shard_map/ppermute | solution.py:26
  52.6 11.4 %collective-permute-start.18 = (bf16[32,1024]{1,0:T(8,128)(2,1)S(1)}, bf16[32,1024]{1,0:T(8,128)(2,1)S(1)}, u32[]{:S(2)}, u32[]{:S(2)}) collective-permute-start(bf16[32,1024]{1,0:T(8,128)(2,1)S(1)} %get-tuple-element.40), channel_id=1, source_target_pairs={{0,20},{4,16},{8,28},{12,24},{16,4},{20,0},{24,12},{28,8},{1,21},{... | collective-permute-start | bytes 196616 | tf_op jit(solution)/shard_map/ppermute | solution.py:26
  52.6 11.4 %collective-permute-start.19 = (bf16[32,1024]{1,0:T(8,128)(2,1)S(1)}, bf16[32,1024]{1,0:T(8,128)(2,1)S(1)}, u32[]{:S(2)}, u32[]{:S(2)}) collective-permute-start(bf16[32,1024]{1,0:T(8,128)(2,1)S(1)} %get-tuple-element.41), channel_id=1, source_target_pairs={{0,16},{4,20},{8,24},{12,28},{16,0},{20,4},{24,8},{28,12},{1,17},{... | collective-permute-start | bytes 196616 | tf_op jit(solution)/shard_map/ppermute | solution.py:26
  56.0 3.5 %copy-start.8 = (bf16[512,1024]{1,0:T(8,128)(2,1)}, bf16[512,1024]{1,0:T(8,128)(2,1)S(1)}, u32[]{:S(2)}) copy-start(bf16[512,1024]{1,0:T(8,128)(2,1)S(1)} %collective-permute-done.15.refs_13_) | copy-start | bytes 3145732
  56.0 8.1 %collective-permute-start.20 = (bf16[32,1024]{1,0:T(8,128)(2,1)S(1)}, bf16[32,1024]{1,0:T(8,128)(2,1)S(1)}, u32[]{:S(2)}, u32[]{:S(2)}) collective-permute-start(bf16[32,1024]{1,0:T(8,128)(2,1)S(1)} %get-tuple-element.43), channel_id=1, source_target_pairs={{0,12},{4,8},{8,4},{12,0},{16,28},{20,24},{24,20},{28,16},{1,13},{... | collective-permute-start | bytes 196616 | tf_op jit(solution)/shard_map/ppermute | solution.py:26
  56.3 7.8 %collective-permute-start.21 = (bf16[32,1024]{1,0:T(8,128)(2,1)S(1)}, bf16[32,1024]{1,0:T(8,128)(2,1)S(1)}, u32[]{:S(2)}, u32[]{:S(2)}) collective-permute-start(bf16[32,1024]{1,0:T(8,128)(2,1)S(1)} %get-tuple-element.44), channel_id=1, source_target_pairs={{0,8},{4,12},{8,0},{12,4},{16,24},{20,28},{24,16},{28,20},{1,9},{5... | collective-permute-start | bytes 196616 | tf_op jit(solution)/shard_map/ppermute | solution.py:26
  58.5 5.6 %collective-permute-start.22 = (bf16[32,1024]{1,0:T(8,128)(2,1)S(1)}, bf16[32,1024]{1,0:T(8,128)(2,1)S(1)}, u32[]{:S(2)}, u32[]{:S(2)}) collective-permute-start(bf16[32,1024]{1,0:T(8,128)(2,1)S(1)} %get-tuple-element.45), channel_id=1, source_target_pairs={{0,4},{4,0},{8,12},{12,8},{16,20},{20,16},{24,28},{28,24},{1,5},{5... | collective-permute-start | bytes 196616 | tf_op jit(solution)/shard_map/ppermute | solution.py:26

commit v2 on v1

--- a/solution.py
+++ b/solution.py
@@ -271,10 +271,11 @@
 
     wide = sds((tokens, width), BF16)
     table, tables, hop = asked, [], n // 2
-    while hop:
+    while hop > 2:
         table = table + exchange(table, "adapter", hop)
         tables.append(table)
         hop //= 2
+    table = table + sum(exchange(table, "adapter", k) for k in (2, 3, 1))
     far_other = product(3, asked, loads=True)
     far_got = exchange(far_other, "tensor", 1)
     near_other = product(1, far_other, loads=False)

time: 65.6 us -> 65 us (level)
  starting transfers between devices: 36.2 us -> 33.6 us
  waiting for transfers between devices: 9.59 us -> 11.6 us
    ppermute x23 -> x24, starting transfers between devices: 36.2 us -> 33.6 us  [exchange(): lax.ppermute(x, axis, [(i, i ^ k) for i in range(lax.axis_size(axis))])]
    ppermute x23 -> x24, waiting for transfers between devices: 9.59 us -> 11.6 us  [exchange(): lax.ppermute(x, axis, [(i, i ^ k) for i in range(lax.axis_size(axis))])]
  transfers between devices with their start and end apart: 23 -> 24, of which waited for: 8 -> 10; matrix products, arithmetic and copies ran while one was open for 0% -> 0% of each run, Pallas kernels for 15% -> 15%
where the time goes in v2:
time: 65 us; the launch traced here: 64.8 us
  starting transfers between devices  33.6 us (52%)
  Pallas kernels  17.9 us (28%)
  waiting for transfers between devices  11.6 us (18%)
  local copies, waits for them, and re-layouts  0.98 us (2%)
  between operations  0.83 us (1%)
    ppermute x24, starting transfers between devices, exchange(): lax.ppermute(x, axis, [(i, i ^ k) for i in range(lax.axis_size(axis))])  33.6 us
    pallas_call x9, Pallas kernels, run(): pl.pallas_call(wrapped, name=getattr(body, 'func', body).__name__, out_sh...  17.9 us
    ppermute x24, waiting for transfers between devices, exchange(): lax.ppermute(x, axis, [(i, i ^ k) for i in range(lax.axis_size(axis))])  11.6 us
  transfers between devices with their start and end apart: 24, of which 10 were waited for; matrix products, arithmetic and copies ran while one was open for 0% of the time, Pallas kernels for 15%

profile of v2, /device:TPU:0, one launch (start us, length us, event | category | flops | bytes accessed | tf_op | source)
XLA Modules:
  0.0 64.8 jit_solution(2617877390910173167)
XLA Ops:
  0.6 0.7 %request_body.1 = (s32[8,128]{1,0:T(8,128)S(1)}, s32[8,512]{1,0:T(8,128)S(1)}) custom-call(s32[1]{0:T(128)} %bitcast.1.refs_0_, s32[64]{0:T(128)} %refs_1_.6, s32[1,6]{1,0:T(1,128)} %refs_2_.7, s32[1,6]{1,0:T(1,128)} %refs_3_.2), custom_call_target="tpu_custom_call" | custom-call | tf_op jit(solution)/shard_map/request_body/pallas_call | solution.py:41
  1.3 3.1 %base_body.3.refs_3_ = bf16[512,1024]{1,0:T(8,128)(2,1)S(1)} custom-call(s32[1]{0:T(128)} %bitcast.3.refs_0_, bf16[4096,1024]{1,0:T(8,128)(2,1)} %refs_12_.1, bf16[512,1024]{1,0:T(8,128)(2,1)} %refs_11_.1, s32[8,128]{1,0:T(8,128)S(1)} %get-tuple-element.27.refs_3_), custom_call_target="tpu_custom_call" | custom-call | flops 1073741824 | bytes 2097152 | tf_op jit(solution)/shard_map/base_body/pallas_call | solution.py:41
  4.4 0.0 copy-start.1
  4.4 0.0 copy-start
  4.4 0.5 collective-permute-start.4
  5.0 3.7 %collective-permute-start = (s32[8,128]{1,0:T(8,128)S(1)}, s32[8,128]{1,0:T(8,128)S(1)}, u32[]{:S(2)}, u32[]{:S(2)}) collective-permute-start(s32[8,128]{1,0:T(8,128)S(1)} %get-tuple-element.27.refs_3_), channel_id=1, source_target_pairs={{0,16},{4,20},{8,24},{12,28},{16,0},{20,4},{24,8},{28,12},{1,17},{... | collective-permute-start | bytes 12296 | tf_op jit(solution)/shard_map/ppermute | solution.py:26
  8.6 1.6 %collective-permute-done = s32[8,128]{1,0:T(8,128)S(1)} collective-permute-done((s32[8,128]{1,0:T(8,128)S(1)}, s32[8,128]{1,0:T(8,128)S(1)}, u32[]{:S(2)}, u32[]{:S(2)}) %collective-permute-start) | collective-permute-done | bytes 4128 | tf_op jit(solution)/shard_map/ppermute | solution.py:26
  10.2 3.2 %base_body.4.refs_4_ = bf16[512,1024]{1,0:T(8,128)(2,1)S(1)} custom-call(s32[1]{0:T(128)} %bitcast.2.refs_0_, bf16[4096,1024]{1,0:T(8,128)(2,1)} %refs_12_.1, bf16[512,1024]{1,0:T(8,128)(2,1)} %refs_11_.1, bf16[512,1024]{1,0:T(8,128)(2,1)} %collective-permute-done.4.refs_3_, s32[8,128]{1,0:T(8,128)S(1)} %add.12.refs_4_), custom_call_target="tpu_custom_call" | custom-call | flops 1073741824 | bytes 2097152 | tf_op jit(solution)/shard_map/base_body/pallas_call | solution.py:41
  13.4 1.9 %collective-permute-start.15 = (bf16[512,1024]{1,0:T(8,128)(2,1)S(1)}, bf16[512,1024]{1,0:T(8,128)(2,1)}, u32[]{:S(2)}, u32[]{:S(2)}) collective-permute-start(bf16[512,1024]{1,0:T(8,128)(2,1)S(1)} %base_body.4.refs_4_), channel_id=1, source_target_pairs={{0,2},{1,3},{2,0},{3,1},{4,6},{5,7},{6,4},{7,5},{8,10},{9,11},{10,... | collective-permute-start | bytes 3145736 | tf_op jit(solution)/shard_map/ppermute | solution.py:26
  15.3 1.5 %collective-permute-start.3 = (s32[8,128]{1,0:T(8,128)S(1)}, s32[8,128]{1,0:T(8,128)S(1)}, u32[]{:S(2)}, u32[]{:S(2)}) collective-permute-start(s32[8,128]{1,0:T(8,128)S(1)} %add.12.refs_4_), channel_id=1, source_target_pairs={{0,4},{4,0},{8,12},{12,8},{16,20},{20,16},{24,28},{28,24},{1,5},{5... | collective-permute-start | bytes 12296 | tf_op jit(solution)/shard_map/ppermute | solution.py:26
  16.8 1.6 %collective-permute-start.2 = (s32[8,128]{1,0:T(8,128)S(1)}, s32[8,128]{1,0:T(8,128)S(1)}, u32[]{:S(2)}, u32[]{:S(2)}) collective-permute-start(s32[8,128]{1,0:T(8,128)S(1)} %add.12.refs_4_), channel_id=1, source_target_pairs={{0,12},{4,8},{8,4},{12,0},{16,28},{20,24},{24,20},{28,16},{1,13},{... | collective-permute-start | bytes 12296 | tf_op jit(solution)/shard_map/ppermute | solution.py:26
  18.4 0.4 collective-permute-start.1
  18.8 0.1 collective-permute-done.3
  18.9 2.4 %collective-permute-done.2 = s32[8,128]{1,0:T(8,128)S(1)} collective-permute-done((s32[8,128]{1,0:T(8,128)S(1)}, s32[8,128]{1,0:T(8,128)S(1)}, u32[]{:S(2)}, u32[]{:S(2)}) %collective-permute-start.2) | collective-permute-done | bytes 4128 | tf_op jit(solution)/shard_map/ppermute | solution.py:26
  21.3 0.7 %collective-permute-done.1 = s32[8,128]{1,0:T(8,128)S(1)} collective-permute-done((s32[8,128]{1,0:T(8,128)S(1)}, s32[8,128]{1,0:T(8,128)S(1)}, u32[]{:S(2)}, u32[]{:S(2)}) %collective-permute-start.1) | collective-permute-done | bytes 4128 | tf_op jit(solution)/shard_map/ppermute | solution.py:26
  22.0 0.9 %copy-done.2 = bf16[128,1024]{1,0:T(8,128)(2,1)S(1)} copy-done((bf16[128,1024]{1,0:T(8,128)(2,1)S(1)}, bf16[128,1024]{1,0:T(8,128)(2,1)}, u32[]{:S(2)}) %copy-start.2) | copy-done | bytes 262168
  22.9 1.0 %select_body.1 = (bf16[32,1024]{1,0:T(8,128)(2,1)}, bf16[32,1024]{1,0:T(8,128)(2,1)}, bf16[32,1024]{1,0:T(8,128)(2,1)}, bf16[32,1024]{1,0:T(8,128)(2,1)S(1)}, bf...) custom-call(s32[1]{0:T(128)} %bitcast.1.refs_0_, ...), custom_call_target="tpu_custom_call" | custom-call | tf_op jit(solution)/shard_map/select_body/pallas_call | solution.py:41
  24.0 3.5 %collective-permute-start.5 = (bf16[32,1024]{1,0:T(8,128)(2,1)}, bf16[32,1024]{1,0:T(8,128)(2,1)S(1)}, u32[]{:S(2)}, u32[]{:S(2)}) collective-permute-start(bf16[32,1024]{1,0:T(8,128)(2,1)} %get-tuple-element.28), channel_id=1, source_target_pairs={{0,28},{4,24},{8,20},{12,16},{16,12},{20,8},{24,4},{28,0},{1,29},{... | collective-permute-start | bytes 196616 | tf_op jit(solution)/shard_map/ppermute | solution.py:26
  27.4 1.3 %collective-permute-start.6 = (bf16[32,1024]{1,0:T(8,128)(2,1)}, bf16[32,1024]{1,0:T(8,128)(2,1)S(1)}, u32[]{:S(2)}, u32[]{:S(2)}) collective-permute-start(bf16[32,1024]{1,0:T(8,128)(2,1)} %get-tuple-element.29), channel_id=1, source_target_pairs={{0,24},{4,28},{8,16},{12,20},{16,8},{20,12},{24,0},{28,4},{1,25},{... | collective-permute-start | bytes 196616 | tf_op jit(solution)/shard_map/ppermute | solution.py:26
  28.8 0.8 %collective-permute-start.7 = (bf16[32,1024]{1,0:T(8,128)(2,1)}, bf16[32,1024]{1,0:T(8,128)(2,1)S(1)}, u32[]{:S(2)}, u32[]{:S(2)}) collective-permute-start(bf16[32,1024]{1,0:T(8,128)(2,1)} %get-tuple-element.30), channel_id=1, source_target_pairs={{0,20},{4,16},{8,28},{12,24},{16,4},{20,0},{24,12},{28,8},{1,21},{... | collective-permute-start | bytes 196616 | tf_op jit(solution)/shard_map/ppermute | solution.py:26
  29.6 2.1 %collective-permute-start.8 = (bf16[32,1024]{1,0:T(8,128)(2,1)}, bf16[32,1024]{1,0:T(8,128)(2,1)S(1)}, u32[]{:S(2)}, u32[]{:S(2)}) collective-permute-start(bf16[32,1024]{1,0:T(8,128)(2,1)} %copy-done.7), channel_id=1, source_target_pairs={{0,16},{4,20},{8,24},{12,28},{16,0},{20,4},{24,8},{28,12},{1,17},{... | collective-permute-start | bytes 196616 | tf_op jit(solution)/shard_map/ppermute | solution.py:26
  31.7 0.2 collective-permute-done.5.refs_3_
  31.9 1.4 %collective-permute-start.9 = (bf16[32,1024]{1,0:T(8,128)(2,1)}, bf16[32,1024]{1,0:T(8,128)(2,1)S(1)}, u32[]{:S(2)}, u32[]{:S(2)}) collective-permute-start(bf16[32,1024]{1,0:T(8,128)(2,1)} %copy-done.6), channel_id=1, source_target_pairs={{0,12},{4,8},{8,4},{12,0},{16,28},{20,24},{24,20},{28,16},{1,13},{... | collective-permute-start | bytes 196616 | tf_op jit(solution)/shard_map/ppermute | solution.py:26
  33.3 1.0 %collective-permute-done.6.refs_4_ = bf16[32,1024]{1,0:T(8,128)(2,1)S(1)} collective-permute-done((bf16[32,1024]{1,0:T(8,128)(2,1)}, bf16[32,1024]{1,0:T(8,128)(2,1)S(1)}, u32[]{:S(2)}, u32[]{:S(2)}) %collective-permute-start.6) | collective-permute-done | bytes 65568 | tf_op jit(solution)/shard_map/ppermute | solution.py:26
  34.4 1.4 %collective-permute-start.10 = (bf16[32,1024]{1,0:T(8,128)(2,1)}, bf16[32,1024]{1,0:T(8,128)(2,1)S(1)}, u32[]{:S(2)}, u32[]{:S(2)}) collective-permute-start(bf16[32,1024]{1,0:T(8,128)(2,1)} %copy-done.5), channel_id=1, source_target_pairs={{0,8},{4,12},{8,0},{12,4},{16,24},{20,28},{24,16},{28,20},{1,9},{5... | collective-permute-start | bytes 196616 | tf_op jit(solution)/shard_map/ppermute | solution.py:26
  35.8 2.0 %collective-permute-done.7.refs_5_ = bf16[32,1024]{1,0:T(8,128)(2,1)S(1)} collective-permute-done((bf16[32,1024]{1,0:T(8,128)(2,1)}, bf16[32,1024]{1,0:T(8,128)(2,1)S(1)}, u32[]{:S(2)}, u32[]{:S(2)}) %collective-permute-start.7) | collective-permute-done | bytes 65568 | tf_op jit(solution)/shard_map/ppermute | solution.py:26
  37.7 0.2 collective-permute-start.11
  37.9 2.7 %base_body.5 = bf16[512,1024]{1,0:T(8,128)(2,1)S(1)} custom-call(s32[1]{0:T(128)} %bitcast.4.refs_0_, bf16[512,1024]{1,0:T(8,128)(2,1)S(1)} %copy-done, bf16[4096,1024]{1,0:T(8,128)(2,1)} %refs_12_.1, bf16[512,1024]{1,0:T(8,128)(2,1)S(1)} %base_body.3.refs_3_), custom_call_target="tpu_custom_call" | custom-call | flops 1073741824 | bytes 2097152 | tf_op jit(solution)/shard_map/base_body/pallas_call | solution.py:41
  40.7 0.1 collective-permute-start.16
  40.8 1.4 %collective-permute-done.11.refs_10_ = bf16[32,1024]{1,0:T(8,128)(2,1)S(1)} collective-permute-done((bf16[32,1024]{1,0:T(8,128)(2,1)}, bf16[32,1024]{1,0:T(8,128)(2,1)S(1)}, u32[]{:S(2)}, u32[]{:S(2)}) %collective-permute-start.11) | collective-permute-done | bytes 65568 | tf_op jit(solution)/shard_map/ppermute | solution.py:26
  42.2 0.8 %project_body.1.refs_3_ = bf16[32,512]{1,0:T(8,128)(2,1)S(1)} custom-call(s32[8,512]{1,0:T(8,128)S(1)} %get-tuple-element.26.refs_0_.refs_1_, bf16[512,1024]{1,0:T(8,128)(2,1)S(1)} %copy-done.3, bf16[512,1024]{1,0:T(8,128)(2,1)S(1)} %copy-done, bf16[32,1024]{1,0:T(8,128)(2,1)S(1)} %collective-permute-done.5.refs_3_, ...), custom_call_target="tpu_custom_call" | custom-call | flops 5000000000 | tf_op jit(solution)/shard_map/project_body/pallas_call | solution.py:41
  43.0 0.1 collective-permute-start.14
  43.1 0.7 %collective-permute-start.13 = (bf16[32,512]{1,0:T(8,128)(2,1)S(1)}, bf16[32,512]{1,0:T(8,128)(2,1)S(1)}, u32[]{:S(2)}, u32[]{:S(2)}) collective-permute-start(bf16[32,512]{1,0:T(8,128)(2,1)S(1)} %project_body.1.refs_3_), channel_id=1, source_target_pairs={{0,2},{1,3},{2,0},{3,1},{4,6},{5,7},{6,4},{7,5},{8,10},{9,11},{10,... | collective-permute-start | bytes 98312 | tf_op jit(solution)/shard_map/ppermute | solution.py:26
  43.8 1.2 %collective-permute-start.12 = (bf16[32,512]{1,0:T(8,128)(2,1)S(1)}, bf16[32,512]{1,0:T(8,128)(2,1)S(1)}, u32[]{:S(2)}, u32[]{:S(2)}) collective-permute-start(bf16[32,512]{1,0:T(8,128)(2,1)S(1)} %project_body.1.refs_3_), channel_id=1, source_target_pairs={{0,1},{1,0},{2,3},{3,2},{4,5},{5,4},{6,7},{7,6},{8,9},{9,8},{10,11... | collective-permute-start | bytes 98312 | tf_op jit(solution)/shard_map/ppermute | solution.py:26
  45.0 1.5 %collective-permute-done.14.refs_6_ = bf16[32,512]{1,0:T(8,128)(2,1)S(1)} collective-permute-done((bf16[32,512]{1,0:T(8,128)(2,1)S(1)}, bf16[32,512]{1,0:T(8,128)(2,1)S(1)}, u32[]{:S(2)}, u32[]{:S(2)}) %collective-permute-start.14) | collective-permute-done | bytes 32800 | tf_op jit(solution)/shard_map/ppermute | solution.py:26
  46.4 0.7 %collective-permute-done.13.refs_5_ = bf16[32,512]{1,0:T(8,128)(2,1)S(1)} collective-permute-done((bf16[32,512]{1,0:T(8,128)(2,1)S(1)}, bf16[32,512]{1,0:T(8,128)(2,1)S(1)}, u32[]{:S(2)}, u32[]{:S(2)}) %collective-permute-start.13) | collective-permute-done | bytes 32800 | tf_op jit(solution)/shard_map/ppermute | solution.py:26
  47.2 0.0 collective-permute-done.12.refs_4_
  47.2 0.0 collective-permute-done.15.refs_7_.refs_14_
  47.2 0.5 gradient_body.1
  47.6 3.2 %collective-permute-start.17 = (bf16[32,1024]{1,0:T(8,128)(2,1)S(1)}, bf16[32,1024]{1,0:T(8,128)(2,1)S(1)}, u32[]{:S(2)}, u32[]{:S(2)}) collective-permute-start(bf16[32,1024]{1,0:T(8,128)(2,1)S(1)} %get-tuple-element.38), channel_id=1, source_target_pairs={{0,28},{4,24},{8,20},{12,16},{16,12},{20,8},{24,4},{28,0},{1,29},{... | collective-permute-start | bytes 196616 | tf_op jit(solution)/shard_map/ppermute | solution.py:26
  50.8 1.0 %collective-permute-start.18 = (bf16[32,1024]{1,0:T(8,128)(2,1)S(1)}, bf16[32,1024]{1,0:T(8,128)(2,1)S(1)}, u32[]{:S(2)}, u32[]{:S(2)}) collective-permute-start(bf16[32,1024]{1,0:T(8,128)(2,1)S(1)} %get-tuple-element.39), channel_id=1, source_target_pairs={{0,24},{4,28},{8,16},{12,20},{16,8},{20,12},{24,0},{28,4},{1,25},{... | collective-permute-start | bytes 196616 | tf_op jit(solution)/shard_map/ppermute | solution.py:26
  51.8 3.5 %collective-permute-start.20 = (bf16[32,1024]{1,0:T(8,128)(2,1)S(1)}, bf16[32,1024]{1,0:T(8,128)(2,1)S(1)}, u32[]{:S(2)}, u32[]{:S(2)}) collective-permute-start(bf16[32,1024]{1,0:T(8,128)(2,1)S(1)} %get-tuple-element.41), channel_id=1, source_target_pairs={{0,16},{4,20},{8,24},{12,28},{16,0},{20,4},{24,8},{28,12},{1,17},{... | collective-permute-start | bytes 196616 | tf_op jit(solution)/shard_map/ppermute | solution.py:26
  55.3 0.8 %collective-permute-start.21 = (bf16[32,1024]{1,0:T(8,128)(2,1)S(1)}, bf16[32,1024]{1,0:T(8,128)(2,1)S(1)}, u32[]{:S(2)}, u32[]{:S(2)}) collective-permute-start(bf16[32,1024]{1,0:T(8,128)(2,1)S(1)} %get-tuple-element.43), channel_id=1, source_target_pairs={{0,12},{4,8},{8,4},{12,0},{16,28},{20,24},{24,20},{28,16},{1,13},{... | collective-permute-start | bytes 196616 | tf_op jit(solution)/shard_map/ppermute | solution.py:26
  56.1 1.5 %collective-permute-start.22 = (bf16[32,1024]{1,0:T(8,128)(2,1)S(1)}, bf16[32,1024]{1,0:T(8,128)(2,1)S(1)}, u32[]{:S(2)}, u32[]{:S(2)}) collective-permute-start(bf16[32,1024]{1,0:T(8,128)(2,1)S(1)} %get-tuple-element.44), channel_id=1, source_target_pairs={{0,8},{4,12},{8,0},{12,4},{16,24},{20,28},{24,16},{28,20},{1,9},{5... | collective-permute-start | bytes 196616 | tf_op jit(solution)/shard_map/ppermute | solution.py:26
  57.7 0.0 collective-permute-done.18.refs_3_
  57.7 1.2 %collective-permute-start.23 = (bf16[32,1024]{1,0:T(8,128)(2,1)S(1)}, bf16[32,1024]{1,0:T(8,128)(2,1)S(1)}, u32[]{:S(2)}, u32[]{:S(2)}) collective-permute-start(bf16[32,1024]{1,0:T(8,128)(2,1)S(1)} %get-tuple-element.45), channel_id=1, source_target_pairs={{0,4},{4,0},{8,12},{12,8},{16,20},{20,16},{24,28},{28,24},{1,5},{5... | collective-permute-start | bytes 196616 | tf_op jit(solution)/shard_map/ppermute | solution.py:26
  58.8 4.6 %finish_body.1 = (bf16[512,1024]{1,0:T(8,128)(2,1)}, f32[8,128]{1,0:T(8,128)S(1)}) custom-call(s32[1]{0:T(128)} %bitcast.refs_0_, s32[8,512]{1,0:T(8,128)S(1)} %get-tuple-element.26.refs_0_.refs_1_, bf16[32,512]{1,0:T(8,128)(2,1)S(1)} %get-tuple-element.36.refs_2_, bf16[32,1024]{1,0:T(8,128)(2,1)S(1)} %collective-permute-done.5.refs_3_, ...), custom_call_target="tpu_custom_call" | custom-call | flops 1073741824 | tf_op jit(solution)/shard_map/finish_body/pallas_call | solution.py:41
  63.5 1.4 %collect_body.1 = (f32[128,1024]{1,0:T(8,128)}, f32[128,1024]{1,0:T(8,128)}) custom-call(s32[1]{0:T(128)} %bitcast.1.refs_0_, s32[8,128]{1,0:T(8,128)S(1)} %add_add_fusion.refs_1_, bf16[32,1024]{1,0:T(8,128)(2,1)S(1)} %collective-permute-done.17.refs_2_, bf16[32,1024]{1,0:T(8,128)(2,1)S(1)} %collective-permute-done.18.refs_3_, ...), custom_call_target="tpu_custom_call" | custom-call | tf_op jit(solution)/shard_map/collect_body/pallas_call | solution.py:41
  (29 shorter events, 0.1 us)
Async XLA Ops:
  4.4 17.6 %copy-start.1 = (bf16[128,1024]{1,0:T(8,128)(2,1)S(1)}, bf16[128,1024]{1,0:T(8,128)(2,1)}, u32[]{:S(2)}) copy-start(bf16[128,1024]{1,0:T(8,128)(2,1)} %refs_2_.10) | copy-start | bytes 786436
  4.4 33.5 %copy-start = (bf16[512,1024]{1,0:T(8,128)(2,1)S(1)}, bf16[512,1024]{1,0:T(8,128)(2,1)}, u32[]{:S(2)}) copy-start(bf16[512,1024]{1,0:T(8,128)(2,1)} %refs_11_.1) | copy-start | bytes 3145732
  4.4 5.8 %collective-permute-start.4 = (bf16[512,1024]{1,0:T(8,128)(2,1)S(1)}, bf16[512,1024]{1,0:T(8,128)(2,1)}, u32[]{:S(2)}, u32[]{:S(2)}) collective-permute-start(bf16[512,1024]{1,0:T(8,128)(2,1)S(1)} %base_body.3.refs_3_), channel_id=1, source_target_pairs={{0,1},{1,0},{2,3},{3,2},{4,5},{5,4},{6,7},{7,6},{8,9},{9,8},{10,11... | collective-permute-start | bytes 3145736 | tf_op jit(solution)/shard_map/ppermute | solution.py:26
  5.0 5.3 %collective-permute-start = (s32[8,128]{1,0:T(8,128)S(1)}, s32[8,128]{1,0:T(8,128)S(1)}, u32[]{:S(2)}, u32[]{:S(2)}) collective-permute-start(s32[8,128]{1,0:T(8,128)S(1)} %get-tuple-element.27.refs_3_), channel_id=1, source_target_pairs={{0,16},{4,20},{8,24},{12,28},{16,0},{20,4},{24,8},{28,12},{1,17},{... | collective-permute-start | bytes 12296 | tf_op jit(solution)/shard_map/ppermute | solution.py:26
  13.4 33.7 %collective-permute-start.15 = (bf16[512,1024]{1,0:T(8,128)(2,1)S(1)}, bf16[512,1024]{1,0:T(8,128)(2,1)}, u32[]{:S(2)}, u32[]{:S(2)}) collective-permute-start(bf16[512,1024]{1,0:T(8,128)(2,1)S(1)} %base_body.4.refs_4_), channel_id=1, source_target_pairs={{0,2},{1,3},{2,0},{3,1},{4,6},{5,7},{6,4},{7,5},{8,10},{9,11},{10,... | collective-permute-start | bytes 3145736 | tf_op jit(solution)/shard_map/ppermute | solution.py:26
  15.3 3.6 %collective-permute-start.3 = (s32[8,128]{1,0:T(8,128)S(1)}, s32[8,128]{1,0:T(8,128)S(1)}, u32[]{:S(2)}, u32[]{:S(2)}) collective-permute-start(s32[8,128]{1,0:T(8,128)S(1)} %add.12.refs_4_), channel_id=1, source_target_pairs={{0,4},{4,0},{8,12},{12,8},{16,20},{20,16},{24,28},{28,24},{1,5},{5... | collective-permute-start | bytes 12296 | tf_op jit(solution)/shard_map/ppermute | solution.py:26
  16.8 4.5 %collective-permute-start.2 = (s32[8,128]{1,0:T(8,128)S(1)}, s32[8,128]{1,0:T(8,128)S(1)}, u32[]{:S(2)}, u32[]{:S(2)}) collective-permute-start(s32[8,128]{1,0:T(8,128)S(1)} %add.12.refs_4_), channel_id=1, source_target_pairs={{0,12},{4,8},{8,4},{12,0},{16,28},{20,24},{24,20},{28,16},{1,13},{... | collective-permute-start | bytes 12296 | tf_op jit(solution)/shard_map/ppermute | solution.py:26
  18.4 3.6 %collective-permute-start.1 = (s32[8,128]{1,0:T(8,128)S(1)}, s32[8,128]{1,0:T(8,128)S(1)}, u32[]{:S(2)}, u32[]{:S(2)}) collective-permute-start(s32[8,128]{1,0:T(8,128)S(1)} %add.12.refs_4_), channel_id=1, source_target_pairs={{0,8},{4,12},{8,0},{12,4},{16,24},{20,28},{24,16},{28,20},{1,9},{5... | collective-permute-start | bytes 12296 | tf_op jit(solution)/shard_map/ppermute | solution.py:26
  22.0 1.0 %copy-start.2 = (bf16[128,1024]{1,0:T(8,128)(2,1)S(1)}, bf16[128,1024]{1,0:T(8,128)(2,1)}, u32[]{:S(2)}) copy-start(bf16[128,1024]{1,0:T(8,128)(2,1)} %refs_3_.3) | copy-start | bytes 786436
  23.9 4.8 %copy-start.4 = (bf16[32,1024]{1,0:T(8,128)(2,1)}, bf16[32,1024]{1,0:T(8,128)(2,1)S(1)}, u32[]{:S(2)}) copy-start(bf16[32,1024]{1,0:T(8,128)(2,1)S(1)} %get-tuple-element.35) | copy-start | bytes 196612
  23.9 4.8 %copy-start.5 = (bf16[32,1024]{1,0:T(8,128)(2,1)}, bf16[32,1024]{1,0:T(8,128)(2,1)S(1)}, u32[]{:S(2)}) copy-start(bf16[32,1024]{1,0:T(8,128)(2,1)S(1)} %get-tuple-element.34) | copy-start | bytes 196612
  23.9 4.8 %copy-start.6 = (bf16[32,1024]{1,0:T(8,128)(2,1)}, bf16[32,1024]{1,0:T(8,128)(2,1)S(1)}, u32[]{:S(2)}) copy-start(bf16[32,1024]{1,0:T(8,128)(2,1)S(1)} %get-tuple-element.33) | copy-start | bytes 196612
  23.9 4.8 %copy-start.7 = (bf16[32,1024]{1,0:T(8,128)(2,1)}, bf16[32,1024]{1,0:T(8,128)(2,1)S(1)}, u32[]{:S(2)}) copy-start(bf16[32,1024]{1,0:T(8,128)(2,1)S(1)} %get-tuple-element.31) | copy-start | bytes 196612
  24.0 8.0 %collective-permute-start.5 = (bf16[32,1024]{1,0:T(8,128)(2,1)}, bf16[32,1024]{1,0:T(8,128)(2,1)S(1)}, u32[]{:S(2)}, u32[]{:S(2)}) collective-permute-start(bf16[32,1024]{1,0:T(8,128)(2,1)} %get-tuple-element.28), channel_id=1, source_target_pairs={{0,28},{4,24},{8,20},{12,16},{16,12},{20,8},{24,4},{28,0},{1,29},{... | collective-permute-start | bytes 196616 | tf_op jit(solution)/shard_map/ppermute | solution.py:26
  27.4 6.9 %collective-permute-start.6 = (bf16[32,1024]{1,0:T(8,128)(2,1)}, bf16[32,1024]{1,0:T(8,128)(2,1)S(1)}, u32[]{:S(2)}, u32[]{:S(2)}) collective-permute-start(bf16[32,1024]{1,0:T(8,128)(2,1)} %get-tuple-element.29), channel_id=1, source_target_pairs={{0,24},{4,28},{8,16},{12,20},{16,8},{20,12},{24,0},{28,4},{1,25},{... | collective-permute-start | bytes 196616 | tf_op jit(solution)/shard_map/ppermute | solution.py:26
  28.8 9.0 %collective-permute-start.7 = (bf16[32,1024]{1,0:T(8,128)(2,1)}, bf16[32,1024]{1,0:T(8,128)(2,1)S(1)}, u32[]{:S(2)}, u32[]{:S(2)}) collective-permute-start(bf16[32,1024]{1,0:T(8,128)(2,1)} %get-tuple-element.30), channel_id=1, source_target_pairs={{0,20},{4,16},{8,28},{12,24},{16,4},{20,0},{24,12},{28,8},{1,21},{... | collective-permute-start | bytes 196616 | tf_op jit(solution)/shard_map/ppermute | solution.py:26
  29.6 12.6 %copy-start.3 = (bf16[512,1024]{1,0:T(8,128)(2,1)S(1)}, bf16[512,1024]{1,0:T(8,128)(2,1)}, u32[]{:S(2)}) copy-start(bf16[512,1024]{1,0:T(8,128)(2,1)} %refs_1_.10) | copy-start | bytes 3145732
  29.6 11.1 %collective-permute-start.8 = (bf16[32,1024]{1,0:T(8,128)(2,1)}, bf16[32,1024]{1,0:T(8,128)(2,1)S(1)}, u32[]{:S(2)}, u32[]{:S(2)}) collective-permute-start(bf16[32,1024]{1,0:T(8,128)(2,1)} %copy-done.7), channel_id=1, source_target_pairs={{0,16},{4,20},{8,24},{12,28},{16,0},{20,4},{24,8},{28,12},{1,17},{... | collective-permute-start | bytes 196616 | tf_op jit(solution)/shard_map/ppermute | solution.py:26
  31.9 8.8 %collective-permute-start.9 = (bf16[32,1024]{1,0:T(8,128)(2,1)}, bf16[32,1024]{1,0:T(8,128)(2,1)S(1)}, u32[]{:S(2)}, u32[]{:S(2)}) collective-permute-start(bf16[32,1024]{1,0:T(8,128)(2,1)} %copy-done.6), channel_id=1, source_target_pairs={{0,12},{4,8},{8,4},{12,0},{16,28},{20,24},{24,20},{28,16},{1,13},{... | collective-permute-start | bytes 196616 | tf_op jit(solution)/shard_map/ppermute | solution.py:26
  34.4 6.4 %collective-permute-start.10 = (bf16[32,1024]{1,0:T(8,128)(2,1)}, bf16[32,1024]{1,0:T(8,128)(2,1)S(1)}, u32[]{:S(2)}, u32[]{:S(2)}) collective-permute-start(bf16[32,1024]{1,0:T(8,128)(2,1)} %copy-done.5), channel_id=1, source_target_pairs={{0,8},{4,12},{8,0},{12,4},{16,24},{20,28},{24,16},{28,20},{1,9},{5... | collective-permute-start | bytes 196616 | tf_op jit(solution)/shard_map/ppermute | solution.py:26
  37.7 4.5 %collective-permute-start.11 = (bf16[32,1024]{1,0:T(8,128)(2,1)}, bf16[32,1024]{1,0:T(8,128)(2,1)S(1)}, u32[]{:S(2)}, u32[]{:S(2)}) collective-permute-start(bf16[32,1024]{1,0:T(8,128)(2,1)} %copy-done.4), channel_id=1, source_target_pairs={{0,4},{4,0},{8,12},{12,8},{16,20},{20,16},{24,28},{28,24},{1,5},{5... | collective-permute-start | bytes 196616 | tf_op jit(solution)/shard_map/ppermute | solution.py:26
  40.7 14.6 %collective-permute-start.16 = (bf16[512,1024]{1,0:T(8,128)(2,1)S(1)}, bf16[512,1024]{1,0:T(8,128)(2,1)S(1)}, u32[]{:S(2)}, u32[]{:S(2)}) collective-permute-start(bf16[512,1024]{1,0:T(8,128)(2,1)S(1)} %base_body.5), channel_id=1, source_target_pairs={{0,1},{1,0},{2,3},{3,2},{4,5},{5,4},{6,7},{7,6},{8,9},{9,8},{10,11... | collective-permute-start | bytes 3145736 | tf_op jit(solution)/shard_map/ppermute | solution.py:26
  43.0 3.4 %collective-permute-start.14 = (bf16[32,512]{1,0:T(8,128)(2,1)S(1)}, bf16[32,512]{1,0:T(8,128)(2,1)S(1)}, u32[]{:S(2)}, u32[]{:S(2)}) collective-permute-start(bf16[32,512]{1,0:T(8,128)(2,1)S(1)} %project_body.1.refs_3_), channel_id=1, source_target_pairs={{0,3},{1,2},{2,1},{3,0},{4,7},{5,6},{6,5},{7,4},{8,11},{9,10},{10,... | collective-permute-start | bytes 98312 | tf_op jit(solution)/shard_map/ppermute | solution.py:26
  43.1 4.0 %collective-permute-start.13 = (bf16[32,512]{1,0:T(8,128)(2,1)S(1)}, bf16[32,512]{1,0:T(8,128)(2,1)S(1)}, u32[]{:S(2)}, u32[]{:S(2)}) collective-permute-start(bf16[32,512]{1,0:T(8,128)(2,1)S(1)} %project_body.1.refs_3_), channel_id=1, source_target_pairs={{0,2},{1,3},{2,0},{3,1},{4,6},{5,7},{6,4},{7,5},{8,10},{9,11},{10,... | collective-permute-start | bytes 98312 | tf_op jit(solution)/shard_map/ppermute | solution.py:26
  43.8 3.3 %collective-permute-start.12 = (bf16[32,512]{1,0:T(8,128)(2,1)S(1)}, bf16[32,512]{1,0:T(8,128)(2,1)S(1)}, u32[]{:S(2)}, u32[]{:S(2)}) collective-permute-start(bf16[32,512]{1,0:T(8,128)(2,1)S(1)} %project_body.1.refs_3_), channel_id=1, source_target_pairs={{0,1},{1,0},{2,3},{3,2},{4,5},{5,4},{6,7},{7,6},{8,9},{9,8},{10,11... | collective-permute-start | bytes 98312 | tf_op jit(solution)/shard_map/ppermute | solution.py:26
  47.6 8.5 %collective-permute-start.17 = (bf16[32,1024]{1,0:T(8,128)(2,1)S(1)}, bf16[32,1024]{1,0:T(8,128)(2,1)S(1)}, u32[]{:S(2)}, u32[]{:S(2)}) collective-permute-start(bf16[32,1024]{1,0:T(8,128)(2,1)S(1)} %get-tuple-element.38), channel_id=1, source_target_pairs={{0,28},{4,24},{8,20},{12,16},{16,12},{20,8},{24,4},{28,0},{1,29},{... | collective-permute-start | bytes 196616 | tf_op jit(solution)/shard_map/ppermute | solution.py:26
  50.8 6.9 %collective-permute-start.18 = (bf16[32,1024]{1,0:T(8,128)(2,1)S(1)}, bf16[32,1024]{1,0:T(8,128)(2,1)S(1)}, u32[]{:S(2)}, u32[]{:S(2)}) collective-permute-start(bf16[32,1024]{1,0:T(8,128)(2,1)S(1)} %get-tuple-element.39), channel_id=1, source_target_pairs={{0,24},{4,28},{8,16},{12,20},{16,8},{20,12},{24,0},{28,4},{1,25},{... | collective-permute-start | bytes 196616 | tf_op jit(solution)/shard_map/ppermute | solution.py:26
  51.8 11.6 %collective-permute-start.19 = (bf16[32,1024]{1,0:T(8,128)(2,1)S(1)}, bf16[32,1024]{1,0:T(8,128)(2,1)S(1)}, u32[]{:S(2)}, u32[]{:S(2)}) collective-permute-start(bf16[32,1024]{1,0:T(8,128)(2,1)S(1)} %get-tuple-element.40), channel_id=1, source_target_pairs={{0,20},{4,16},{8,28},{12,24},{16,4},{20,0},{24,12},{28,8},{1,21},{... | collective-permute-start | bytes 196616 | tf_op jit(solution)/shard_map/ppermute | solution.py:26
  51.8 11.6 %collective-permute-start.20 = (bf16[32,1024]{1,0:T(8,128)(2,1)S(1)}, bf16[32,1024]{1,0:T(8,128)(2,1)S(1)}, u32[]{:S(2)}, u32[]{:S(2)}) collective-permute-start(bf16[32,1024]{1,0:T(8,128)(2,1)S(1)} %get-tuple-element.41), channel_id=1, source_target_pairs={{0,16},{4,20},{8,24},{12,28},{16,0},{20,4},{24,8},{28,12},{1,17},{... | collective-permute-start | bytes 196616 | tf_op jit(solution)/shard_map/ppermute | solution.py:26
  55.3 3.5 %copy-start.8 = (bf16[512,1024]{1,0:T(8,128)(2,1)}, bf16[512,1024]{1,0:T(8,128)(2,1)S(1)}, u32[]{:S(2)}) copy-start(bf16[512,1024]{1,0:T(8,128)(2,1)S(1)} %collective-permute-done.16.refs_13_) | copy-start | bytes 3145732
  55.3 8.1 %collective-permute-start.21 = (bf16[32,1024]{1,0:T(8,128)(2,1)S(1)}, bf16[32,1024]{1,0:T(8,128)(2,1)S(1)}, u32[]{:S(2)}, u32[]{:S(2)}) collective-permute-start(bf16[32,1024]{1,0:T(8,128)(2,1)S(1)} %get-tuple-element.43), channel_id=1, source_target_pairs={{0,12},{4,8},{8,4},{12,0},{16,28},{20,24},{24,20},{28,16},{1,13},{... | collective-permute-start | bytes 196616 | tf_op jit(solution)/shard_map/ppermute | solution.py:26
  56.1 7.3 %collective-permute-start.22 = (bf16[32,1024]{1,0:T(8,128)(2,1)S(1)}, bf16[32,1024]{1,0:T(8,128)(2,1)S(1)}, u32[]{:S(2)}, u32[]{:S(2)}) collective-permute-start(bf16[32,1024]{1,0:T(8,128)(2,1)S(1)} %get-tuple-element.44), channel_id=1, source_target_pairs={{0,8},{4,12},{8,0},{12,4},{16,24},{20,28},{24,16},{28,20},{1,9},{5... | collective-permute-start | bytes 196616 | tf_op jit(solution)/shard_map/ppermute | solution.py:26
  57.7 5.8 %collective-permute-start.23 = (bf16[32,1024]{1,0:T(8,128)(2,1)S(1)}, bf16[32,1024]{1,0:T(8,128)(2,1)S(1)}, u32[]{:S(2)}, u32[]{:S(2)}) collective-permute-start(bf16[32,1024]{1,0:T(8,128)(2,1)S(1)} %get-tuple-element.45), channel_id=1, source_target_pairs={{0,4},{4,0},{8,12},{12,8},{16,20},{20,16},{24,28},{28,24},{1,5},{5... | collective-permute-start | bytes 196616 | tf_op jit(solution)/shard_map/ppermute | solution.py:26

commit v3 on v2

--- a/solution.py
+++ b/solution.py
@@ -30,7 +30,7 @@
     return jax.ShapeDtypeStruct(shape, dtype)
 
 
-def call(body, outs, n_vmem, n_smem=0, n_hbm=0, scratch=(), flops=0, moved=0, vmem=16):
+def call(body, outs, n_vmem, n_smem=0, n_hbm=0, scratch=(), flops=0, moved=0, vmem=16, space=VMEM):
     def run(*operands, after=()):
         tokens = len(after)
         at = n_smem + n_vmem + n_hbm
@@ -46,7 +46,7 @@
             + [VMEM] * n_vmem
             + [pl.BlockSpec(memory_space=pltpu.HBM)] * n_hbm
             + [pl.BlockSpec(memory_space=pl.ANY)] * tokens,
-            out_specs=jax.tree.map(lambda _: VMEM, outs),
+            out_specs=jax.tree.map(lambda _: space, outs),
             scratch_shapes=scratch,
             cost_estimate=pl.CostEstimate(flops=flops, bytes_accessed=moved, transcendentals=0),
             compiler_params=pltpu.CompilerParams(vmem_limit_bytes=vmem * 2**20),
@@ -139,7 +139,7 @@
 
 
 def collect_body(ks, me_ref, table_ref, *refs):
-    in_refs, down_ref, up_ref = refs[: len(ks)], refs[-2], refs[-1]
+    in_refs, (down_ref, up_ref, down_sum, up_sum, sems) = refs[: len(ks)], refs[len(ks) :]
     me = me_ref[0]
     table = table_ref[...]
     rows = SLOTS * RANK
@@ -148,10 +148,14 @@
     place = jnp.concatenate(
         [(row == (wanted(me, k, table) - 1) * RANK + col).astype(F32).astype(BF16) for k in ks], axis=1
     )
-    down = jnp.concatenate([r[pl.ds(0, RANK), :] for r in in_refs], axis=0)
-    up = jnp.concatenate([r[pl.ds(RANK, RANK), :] for r in in_refs], axis=0)
-    down_ref[...] = dot(place, down, 1, 0)
-    up_ref[...] = dot(place, up, 1, 0)
+    copies = []
+    for i, (held, out) in enumerate(((down_sum, down_ref), (up_sum, up_ref))):
+        terms = jnp.concatenate([r[pl.ds(i * RANK, RANK), :] for r in in_refs], axis=0)
+        held[...] = dot(place, terms, 1, 0)
+        copies.append(pltpu.make_async_copy(held, out, sems.at[i]))
+        copies[-1].start()
+    for c in copies:
+        c.wait()
 
 
 def base_body(tile, loads, adds, at_ref, *refs):
@@ -325,6 +329,8 @@
         (sds((SLOTS * RANK, width), F32), sds((SLOTS * RANK, width), F32)),
         1 + n,
         1,
+        scratch=[pltpu.VMEM((SLOTS * RANK, width), F32)] * 2 + [pltpu.SemaphoreType.DMA((2,))],
+        space=pl.BlockSpec(memory_space=pltpu.HBM),
     )(me, table, *back, after=(finished,))
     return input_gradient, down_grad, up_grad
 

time: 65 us -> 65 us (level)
  no operation moved by 1% of the time
where the time goes in v3:
time: 65 us; the launch traced here: 64.8 us
  starting transfers between devices  33.6 us (52%)
  Pallas kernels  17.9 us (28%)
  waiting for transfers between devices  11.6 us (18%)
  local copies, waits for them, and re-layouts  0.98 us (2%)
  between operations  0.83 us (1%)
    ppermute x24, starting transfers between devices, exchange(): lax.ppermute(x, axis, [(i, i ^ k) for i in range(lax.axis_size(axis))])  33.6 us
    pallas_call x9, Pallas kernels, run(): pl.pallas_call(wrapped, name=getattr(body, 'func', body).__name__, out_sh...  17.9 us
    ppermute x24, waiting for transfers between devices, exchange(): lax.ppermute(x, axis, [(i, i ^ k) for i in range(lax.axis_size(axis))])  11.6 us
  transfers between devices with their start and end apart: 24, of which 10 were waited for; matrix products, arithmetic and copies ran while one was open for 0% of the time, Pallas kernels for 15%

profile of v3, /device:TPU:0, one launch (start us, length us, event | category | flops | bytes accessed | tf_op | source)
XLA Modules:
  0.0 64.8 jit_solution(10207210976997674492)
XLA Ops:
  0.6 0.7 %request_body.1 = (s32[8,128]{1,0:T(8,128)S(1)}, s32[8,512]{1,0:T(8,128)S(1)}) custom-call(s32[1]{0:T(128)} %bitcast.1.refs_0_, s32[64]{0:T(128)} %refs_1_.6, s32[1,6]{1,0:T(1,128)} %refs_2_.7, s32[1,6]{1,0:T(1,128)} %refs_3_.2), custom_call_target="tpu_custom_call" | custom-call | tf_op jit(solution)/shard_map/request_body/pallas_call | solution.py:41
  1.3 3.1 %base_body.3.refs_3_ = bf16[512,1024]{1,0:T(8,128)(2,1)S(1)} custom-call(s32[1]{0:T(128)} %bitcast.3.refs_0_, bf16[4096,1024]{1,0:T(8,128)(2,1)} %refs_12_.1, bf16[512,1024]{1,0:T(8,128)(2,1)} %refs_11_.1, s32[8,128]{1,0:T(8,128)S(1)} %get-tuple-element.27.refs_3_), custom_call_target="tpu_custom_call" | custom-call | flops 1073741824 | bytes 2097152 | tf_op jit(solution)/shard_map/base_body/pallas_call | solution.py:41
  4.4 0.0 copy-start.1
  4.4 0.0 copy-start
  4.4 0.5 collective-permute-start.4
  5.0 3.7 %collective-permute-start = (s32[8,128]{1,0:T(8,128)S(1)}, s32[8,128]{1,0:T(8,128)S(1)}, u32[]{:S(2)}, u32[]{:S(2)}) collective-permute-start(s32[8,128]{1,0:T(8,128)S(1)} %get-tuple-element.27.refs_3_), channel_id=1, source_target_pairs={{0,16},{4,20},{8,24},{12,28},{16,0},{20,4},{24,8},{28,12},{1,17},{... | collective-permute-start | bytes 12296 | tf_op jit(solution)/shard_map/ppermute | solution.py:26
  8.6 1.6 %collective-permute-done = s32[8,128]{1,0:T(8,128)S(1)} collective-permute-done((s32[8,128]{1,0:T(8,128)S(1)}, s32[8,128]{1,0:T(8,128)S(1)}, u32[]{:S(2)}, u32[]{:S(2)}) %collective-permute-start) | collective-permute-done | bytes 4128 | tf_op jit(solution)/shard_map/ppermute | solution.py:26
  10.2 0.0 collective-permute-done.4.refs_3_
  10.2 3.2 %base_body.4.refs_4_ = bf16[512,1024]{1,0:T(8,128)(2,1)S(1)} custom-call(s32[1]{0:T(128)} %bitcast.2.refs_0_, bf16[4096,1024]{1,0:T(8,128)(2,1)} %refs_12_.1, bf16[512,1024]{1,0:T(8,128)(2,1)} %refs_11_.1, bf16[512,1024]{1,0:T(8,128)(2,1)} %collective-permute-done.4.refs_3_, s32[8,128]{1,0:T(8,128)S(1)} %add.12.refs_4_), custom_call_target="tpu_custom_call" | custom-call | flops 1073741824 | bytes 2097152 | tf_op jit(solution)/shard_map/base_body/pallas_call | solution.py:41
  13.4 1.9 %collective-permute-start.15 = (bf16[512,1024]{1,0:T(8,128)(2,1)S(1)}, bf16[512,1024]{1,0:T(8,128)(2,1)}, u32[]{:S(2)}, u32[]{:S(2)}) collective-permute-start(bf16[512,1024]{1,0:T(8,128)(2,1)S(1)} %base_body.4.refs_4_), channel_id=1, source_target_pairs={{0,2},{1,3},{2,0},{3,1},{4,6},{5,7},{6,4},{7,5},{8,10},{9,11},{10,... | collective-permute-start | bytes 3145736 | tf_op jit(solution)/shard_map/ppermute | solution.py:26
  15.3 1.5 %collective-permute-start.3 = (s32[8,128]{1,0:T(8,128)S(1)}, s32[8,128]{1,0:T(8,128)S(1)}, u32[]{:S(2)}, u32[]{:S(2)}) collective-permute-start(s32[8,128]{1,0:T(8,128)S(1)} %add.12.refs_4_), channel_id=1, source_target_pairs={{0,4},{4,0},{8,12},{12,8},{16,20},{20,16},{24,28},{28,24},{1,5},{5... | collective-permute-start | bytes 12296 | tf_op jit(solution)/shard_map/ppermute | solution.py:26
  16.8 1.6 %collective-permute-start.2 = (s32[8,128]{1,0:T(8,128)S(1)}, s32[8,128]{1,0:T(8,128)S(1)}, u32[]{:S(2)}, u32[]{:S(2)}) collective-permute-start(s32[8,128]{1,0:T(8,128)S(1)} %add.12.refs_4_), channel_id=1, source_target_pairs={{0,12},{4,8},{8,4},{12,0},{16,28},{20,24},{24,20},{28,16},{1,13},{... | collective-permute-start | bytes 12296 | tf_op jit(solution)/shard_map/ppermute | solution.py:26
  18.4 0.4 collective-permute-start.1
  18.8 0.1 collective-permute-done.3
  18.9 2.4 %collective-permute-done.2 = s32[8,128]{1,0:T(8,128)S(1)} collective-permute-done((s32[8,128]{1,0:T(8,128)S(1)}, s32[8,128]{1,0:T(8,128)S(1)}, u32[]{:S(2)}, u32[]{:S(2)}) %collective-permute-start.2) | collective-permute-done | bytes 4128 | tf_op jit(solution)/shard_map/ppermute | solution.py:26
  21.3 0.7 %collective-permute-done.1 = s32[8,128]{1,0:T(8,128)S(1)} collective-permute-done((s32[8,128]{1,0:T(8,128)S(1)}, s32[8,128]{1,0:T(8,128)S(1)}, u32[]{:S(2)}, u32[]{:S(2)}) %collective-permute-start.1) | collective-permute-done | bytes 4128 | tf_op jit(solution)/shard_map/ppermute | solution.py:26
  22.0 0.9 %copy-done.2 = bf16[128,1024]{1,0:T(8,128)(2,1)S(1)} copy-done((bf16[128,1024]{1,0:T(8,128)(2,1)S(1)}, bf16[128,1024]{1,0:T(8,128)(2,1)}, u32[]{:S(2)}) %copy-start.2) | copy-done | bytes 262168
  22.9 1.0 %select_body.1 = (bf16[32,1024]{1,0:T(8,128)(2,1)}, bf16[32,1024]{1,0:T(8,128)(2,1)}, bf16[32,1024]{1,0:T(8,128)(2,1)}, bf16[32,1024]{1,0:T(8,128)(2,1)S(1)}, bf...) custom-call(s32[1]{0:T(128)} %bitcast.1.refs_0_, ...), custom_call_target="tpu_custom_call" | custom-call | tf_op jit(solution)/shard_map/select_body/pallas_call | solution.py:41
  24.0 3.5 %collective-permute-start.5 = (bf16[32,1024]{1,0:T(8,128)(2,1)}, bf16[32,1024]{1,0:T(8,128)(2,1)S(1)}, u32[]{:S(2)}, u32[]{:S(2)}) collective-permute-start(bf16[32,1024]{1,0:T(8,128)(2,1)} %get-tuple-element.28), channel_id=1, source_target_pairs={{0,28},{4,24},{8,20},{12,16},{16,12},{20,8},{24,4},{28,0},{1,29},{... | collective-permute-start | bytes 196616 | tf_op jit(solution)/shard_map/ppermute | solution.py:26
  27.4 1.3 %collective-permute-start.6 = (bf16[32,1024]{1,0:T(8,128)(2,1)}, bf16[32,1024]{1,0:T(8,128)(2,1)S(1)}, u32[]{:S(2)}, u32[]{:S(2)}) collective-permute-start(bf16[32,1024]{1,0:T(8,128)(2,1)} %get-tuple-element.29), channel_id=1, source_target_pairs={{0,24},{4,28},{8,16},{12,20},{16,8},{20,12},{24,0},{28,4},{1,25},{... | collective-permute-start | bytes 196616 | tf_op jit(solution)/shard_map/ppermute | solution.py:26
  28.8 0.8 %collective-permute-start.7 = (bf16[32,1024]{1,0:T(8,128)(2,1)}, bf16[32,1024]{1,0:T(8,128)(2,1)S(1)}, u32[]{:S(2)}, u32[]{:S(2)}) collective-permute-start(bf16[32,1024]{1,0:T(8,128)(2,1)} %get-tuple-element.30), channel_id=1, source_target_pairs={{0,20},{4,16},{8,28},{12,24},{16,4},{20,0},{24,12},{28,8},{1,21},{... | collective-permute-start | bytes 196616 | tf_op jit(solution)/shard_map/ppermute | solution.py:26
  29.6 2.1 %collective-permute-start.8 = (bf16[32,1024]{1,0:T(8,128)(2,1)}, bf16[32,1024]{1,0:T(8,128)(2,1)S(1)}, u32[]{:S(2)}, u32[]{:S(2)}) collective-permute-start(bf16[32,1024]{1,0:T(8,128)(2,1)} %copy-done.7), channel_id=1, source_target_pairs={{0,16},{4,20},{8,24},{12,28},{16,0},{20,4},{24,8},{28,12},{1,17},{... | collective-permute-start | bytes 196616 | tf_op jit(solution)/shard_map/ppermute | solution.py:26
  31.7 0.2 collective-permute-done.5.refs_3_
  31.9 1.4 %collective-permute-start.9 = (bf16[32,1024]{1,0:T(8,128)(2,1)}, bf16[32,1024]{1,0:T(8,128)(2,1)S(1)}, u32[]{:S(2)}, u32[]{:S(2)}) collective-permute-start(bf16[32,1024]{1,0:T(8,128)(2,1)} %copy-done.6), channel_id=1, source_target_pairs={{0,12},{4,8},{8,4},{12,0},{16,28},{20,24},{24,20},{28,16},{1,13},{... | collective-permute-start | bytes 196616 | tf_op jit(solution)/shard_map/ppermute | solution.py:26
  33.3 1.0 %collective-permute-done.6.refs_4_ = bf16[32,1024]{1,0:T(8,128)(2,1)S(1)} collective-permute-done((bf16[32,1024]{1,0:T(8,128)(2,1)}, bf16[32,1024]{1,0:T(8,128)(2,1)S(1)}, u32[]{:S(2)}, u32[]{:S(2)}) %collective-permute-start.6) | collective-permute-done | bytes 65568 | tf_op jit(solution)/shard_map/ppermute | solution.py:26
  34.4 1.4 %collective-permute-start.10 = (bf16[32,1024]{1,0:T(8,128)(2,1)}, bf16[32,1024]{1,0:T(8,128)(2,1)S(1)}, u32[]{:S(2)}, u32[]{:S(2)}) collective-permute-start(bf16[32,1024]{1,0:T(8,128)(2,1)} %copy-done.5), channel_id=1, source_target_pairs={{0,8},{4,12},{8,0},{12,4},{16,24},{20,28},{24,16},{28,20},{1,9},{5... | collective-permute-start | bytes 196616 | tf_op jit(solution)/shard_map/ppermute | solution.py:26
  35.8 2.0 %collective-permute-done.7.refs_5_ = bf16[32,1024]{1,0:T(8,128)(2,1)S(1)} collective-permute-done((bf16[32,1024]{1,0:T(8,128)(2,1)}, bf16[32,1024]{1,0:T(8,128)(2,1)S(1)}, u32[]{:S(2)}, u32[]{:S(2)}) %collective-permute-start.7) | collective-permute-done | bytes 65568 | tf_op jit(solution)/shard_map/ppermute | solution.py:26
  37.7 0.2 collective-permute-start.11
  37.9 2.7 %base_body.5 = bf16[512,1024]{1,0:T(8,128)(2,1)S(1)} custom-call(s32[1]{0:T(128)} %bitcast.4.refs_0_, bf16[512,1024]{1,0:T(8,128)(2,1)S(1)} %copy-done, bf16[4096,1024]{1,0:T(8,128)(2,1)} %refs_12_.1, bf16[512,1024]{1,0:T(8,128)(2,1)S(1)} %base_body.3.refs_3_), custom_call_target="tpu_custom_call" | custom-call | flops 1073741824 | bytes 2097152 | tf_op jit(solution)/shard_map/base_body/pallas_call | solution.py:41
  40.7 0.0 collective-permute-done.8.refs_6_
  40.7 0.1 collective-permute-start.16
  40.8 0.0 collective-permute-done.9.refs_8_
  40.8 1.4 %collective-permute-done.11.refs_10_ = bf16[32,1024]{1,0:T(8,128)(2,1)S(1)} collective-permute-done((bf16[32,1024]{1,0:T(8,128)(2,1)}, bf16[32,1024]{1,0:T(8,128)(2,1)S(1)}, u32[]{:S(2)}, u32[]{:S(2)}) %collective-permute-start.11) | collective-permute-done | bytes 65568 | tf_op jit(solution)/shard_map/ppermute | solution.py:26
  42.2 0.8 %project_body.1.refs_3_ = bf16[32,512]{1,0:T(8,128)(2,1)S(1)} custom-call(s32[8,512]{1,0:T(8,128)S(1)} %get-tuple-element.26.refs_0_.refs_1_, bf16[512,1024]{1,0:T(8,128)(2,1)S(1)} %copy-done.3, bf16[512,1024]{1,0:T(8,128)(2,1)S(1)} %copy-done, bf16[32,1024]{1,0:T(8,128)(2,1)S(1)} %collective-permute-done.5.refs_3_, ...), custom_call_target="tpu_custom_call" | custom-call | flops 5000000000 | tf_op jit(solution)/shard_map/project_body/pallas_call | solution.py:41
  43.0 0.1 collective-permute-start.14
  43.1 0.7 %collective-permute-start.13 = (bf16[32,512]{1,0:T(8,128)(2,1)S(1)}, bf16[32,512]{1,0:T(8,128)(2,1)S(1)}, u32[]{:S(2)}, u32[]{:S(2)}) collective-permute-start(bf16[32,512]{1,0:T(8,128)(2,1)S(1)} %project_body.1.refs_3_), channel_id=1, source_target_pairs={{0,2},{1,3},{2,0},{3,1},{4,6},{5,7},{6,4},{7,5},{8,10},{9,11},{10,... | collective-permute-start | bytes 98312 | tf_op jit(solution)/shard_map/ppermute | solution.py:26
  43.8 1.2 %collective-permute-start.12 = (bf16[32,512]{1,0:T(8,128)(2,1)S(1)}, bf16[32,512]{1,0:T(8,128)(2,1)S(1)}, u32[]{:S(2)}, u32[]{:S(2)}) collective-permute-start(bf16[32,512]{1,0:T(8,128)(2,1)S(1)} %project_body.1.refs_3_), channel_id=1, source_target_pairs={{0,1},{1,0},{2,3},{3,2},{4,5},{5,4},{6,7},{7,6},{8,9},{9,8},{10,11... | collective-permute-start | bytes 98312 | tf_op jit(solution)/shard_map/ppermute | solution.py:26
  45.0 1.5 %collective-permute-done.14.refs_6_ = bf16[32,512]{1,0:T(8,128)(2,1)S(1)} collective-permute-done((bf16[32,512]{1,0:T(8,128)(2,1)S(1)}, bf16[32,512]{1,0:T(8,128)(2,1)S(1)}, u32[]{:S(2)}, u32[]{:S(2)}) %collective-permute-start.14) | collective-permute-done | bytes 32800 | tf_op jit(solution)/shard_map/ppermute | solution.py:26
  46.4 0.7 %collective-permute-done.13.refs_5_ = bf16[32,512]{1,0:T(8,128)(2,1)S(1)} collective-permute-done((bf16[32,512]{1,0:T(8,128)(2,1)S(1)}, bf16[32,512]{1,0:T(8,128)(2,1)S(1)}, u32[]{:S(2)}, u32[]{:S(2)}) %collective-permute-start.13) | collective-permute-done | bytes 32800 | tf_op jit(solution)/shard_map/ppermute | solution.py:26
  47.2 0.5 gradient_body.1
  47.6 3.2 %collective-permute-start.17 = (bf16[32,1024]{1,0:T(8,128)(2,1)S(1)}, bf16[32,1024]{1,0:T(8,128)(2,1)S(1)}, u32[]{:S(2)}, u32[]{:S(2)}) collective-permute-start(bf16[32,1024]{1,0:T(8,128)(2,1)S(1)} %get-tuple-element.38), channel_id=1, source_target_pairs={{0,28},{4,24},{8,20},{12,16},{16,12},{20,8},{24,4},{28,0},{1,29},{... | collective-permute-start | bytes 196616 | tf_op jit(solution)/shard_map/ppermute | solution.py:26
  50.8 1.0 %collective-permute-start.18 = (bf16[32,1024]{1,0:T(8,128)(2,1)S(1)}, bf16[32,1024]{1,0:T(8,128)(2,1)S(1)}, u32[]{:S(2)}, u32[]{:S(2)}) collective-permute-start(bf16[32,1024]{1,0:T(8,128)(2,1)S(1)} %get-tuple-element.39), channel_id=1, source_target_pairs={{0,24},{4,28},{8,16},{12,20},{16,8},{20,12},{24,0},{28,4},{1,25},{... | collective-permute-start | bytes 196616 | tf_op jit(solution)/shard_map/ppermute | solution.py:26
  51.8 3.5 %collective-permute-start.20 = (bf16[32,1024]{1,0:T(8,128)(2,1)S(1)}, bf16[32,1024]{1,0:T(8,128)(2,1)S(1)}, u32[]{:S(2)}, u32[]{:S(2)}) collective-permute-start(bf16[32,1024]{1,0:T(8,128)(2,1)S(1)} %get-tuple-element.41), channel_id=1, source_target_pairs={{0,16},{4,20},{8,24},{12,28},{16,0},{20,4},{24,8},{28,12},{1,17},{... | collective-permute-start | bytes 196616 | tf_op jit(solution)/shard_map/ppermute | solution.py:26
  55.3 0.8 %collective-permute-start.21 = (bf16[32,1024]{1,0:T(8,128)(2,1)S(1)}, bf16[32,1024]{1,0:T(8,128)(2,1)S(1)}, u32[]{:S(2)}, u32[]{:S(2)}) collective-permute-start(bf16[32,1024]{1,0:T(8,128)(2,1)S(1)} %get-tuple-element.43), channel_id=1, source_target_pairs={{0,12},{4,8},{8,4},{12,0},{16,28},{20,24},{24,20},{28,16},{1,13},{... | collective-permute-start | bytes 196616 | tf_op jit(solution)/shard_map/ppermute | solution.py:26
  56.1 1.5 %collective-permute-start.22 = (bf16[32,1024]{1,0:T(8,128)(2,1)S(1)}, bf16[32,1024]{1,0:T(8,128)(2,1)S(1)}, u32[]{:S(2)}, u32[]{:S(2)}) collective-permute-start(bf16[32,1024]{1,0:T(8,128)(2,1)S(1)} %get-tuple-element.44), channel_id=1, source_target_pairs={{0,8},{4,12},{8,0},{12,4},{16,24},{20,28},{24,16},{28,20},{1,9},{5... | collective-permute-start | bytes 196616 | tf_op jit(solution)/shard_map/ppermute | solution.py:26
  57.7 1.2 %collective-permute-start.23 = (bf16[32,1024]{1,0:T(8,128)(2,1)S(1)}, bf16[32,1024]{1,0:T(8,128)(2,1)S(1)}, u32[]{:S(2)}, u32[]{:S(2)}) collective-permute-start(bf16[32,1024]{1,0:T(8,128)(2,1)S(1)} %get-tuple-element.45), channel_id=1, source_target_pairs={{0,4},{4,0},{8,12},{12,8},{16,20},{20,16},{24,28},{28,24},{1,5},{5... | collective-permute-start | bytes 196616 | tf_op jit(solution)/shard_map/ppermute | solution.py:26
  58.8 4.6 %finish_body.1 = (bf16[512,1024]{1,0:T(8,128)(2,1)}, f32[8,128]{1,0:T(8,128)S(1)}) custom-call(s32[1]{0:T(128)} %bitcast.refs_0_, s32[8,512]{1,0:T(8,128)S(1)} %get-tuple-element.26.refs_0_.refs_1_, bf16[32,512]{1,0:T(8,128)(2,1)S(1)} %get-tuple-element.36.refs_2_, bf16[32,1024]{1,0:T(8,128)(2,1)S(1)} %collective-permute-done.5.refs_3_, ...), custom_call_target="tpu_custom_call" | custom-call | flops 1073741824 | tf_op jit(solution)/shard_map/finish_body/pallas_call | solution.py:41
  63.5 1.4 %collect_body.1 = (f32[128,1024]{1,0:T(8,128)}, f32[128,1024]{1,0:T(8,128)}) custom-call(s32[1]{0:T(128)} %bitcast.1.refs_0_, s32[8,128]{1,0:T(8,128)S(1)} %add_add_fusion.refs_1_, bf16[32,1024]{1,0:T(8,128)(2,1)S(1)} %collective-permute-done.17.refs_2_, bf16[32,1024]{1,0:T(8,128)(2,1)S(1)} %collective-permute-done.18.refs_3_, ...), custom_call_target="tpu_custom_call" | custom-call | tf_op jit(solution)/shard_map/collect_body/pallas_call | solution.py:41
  (29 shorter events, 0.1 us)
Async XLA Ops:
  4.4 17.6 %copy-start.1 = (bf16[128,1024]{1,0:T(8,128)(2,1)S(1)}, bf16[128,1024]{1,0:T(8,128)(2,1)}, u32[]{:S(2)}) copy-start(bf16[128,1024]{1,0:T(8,128)(2,1)} %refs_2_.10) | copy-start | bytes 786436
  4.4 33.5 %copy-start = (bf16[512,1024]{1,0:T(8,128)(2,1)S(1)}, bf16[512,1024]{1,0:T(8,128)(2,1)}, u32[]{:S(2)}) copy-start(bf16[512,1024]{1,0:T(8,128)(2,1)} %refs_11_.1) | copy-start | bytes 3145732
  4.4 5.8 %collective-permute-start.4 = (bf16[512,1024]{1,0:T(8,128)(2,1)S(1)}, bf16[512,1024]{1,0:T(8,128)(2,1)}, u32[]{:S(2)}, u32[]{:S(2)}) collective-permute-start(bf16[512,1024]{1,0:T(8,128)(2,1)S(1)} %base_body.3.refs_3_), channel_id=1, source_target_pairs={{0,1},{1,0},{2,3},{3,2},{4,5},{5,4},{6,7},{7,6},{8,9},{9,8},{10,11... | collective-permute-start | bytes 3145736 | tf_op jit(solution)/shard_map/ppermute | solution.py:26
  5.0 5.3 %collective-permute-start = (s32[8,128]{1,0:T(8,128)S(1)}, s32[8,128]{1,0:T(8,128)S(1)}, u32[]{:S(2)}, u32[]{:S(2)}) collective-permute-start(s32[8,128]{1,0:T(8,128)S(1)} %get-tuple-element.27.refs_3_), channel_id=1, source_target_pairs={{0,16},{4,20},{8,24},{12,28},{16,0},{20,4},{24,8},{28,12},{1,17},{... | collective-permute-start | bytes 12296 | tf_op jit(solution)/shard_map/ppermute | solution.py:26
  13.4 33.7 %collective-permute-start.15 = (bf16[512,1024]{1,0:T(8,128)(2,1)S(1)}, bf16[512,1024]{1,0:T(8,128)(2,1)}, u32[]{:S(2)}, u32[]{:S(2)}) collective-permute-start(bf16[512,1024]{1,0:T(8,128)(2,1)S(1)} %base_body.4.refs_4_), channel_id=1, source_target_pairs={{0,2},{1,3},{2,0},{3,1},{4,6},{5,7},{6,4},{7,5},{8,10},{9,11},{10,... | collective-permute-start | bytes 3145736 | tf_op jit(solution)/shard_map/ppermute | solution.py:26
  15.3 3.6 %collective-permute-start.3 = (s32[8,128]{1,0:T(8,128)S(1)}, s32[8,128]{1,0:T(8,128)S(1)}, u32[]{:S(2)}, u32[]{:S(2)}) collective-permute-start(s32[8,128]{1,0:T(8,128)S(1)} %add.12.refs_4_), channel_id=1, source_target_pairs={{0,4},{4,0},{8,12},{12,8},{16,20},{20,16},{24,28},{28,24},{1,5},{5... | collective-permute-start | bytes 12296 | tf_op jit(solution)/shard_map/ppermute | solution.py:26
  16.8 4.5 %collective-permute-start.2 = (s32[8,128]{1,0:T(8,128)S(1)}, s32[8,128]{1,0:T(8,128)S(1)}, u32[]{:S(2)}, u32[]{:S(2)}) collective-permute-start(s32[8,128]{1,0:T(8,128)S(1)} %add.12.refs_4_), channel_id=1, source_target_pairs={{0,12},{4,8},{8,4},{12,0},{16,28},{20,24},{24,20},{28,16},{1,13},{... | collective-permute-start | bytes 12296 | tf_op jit(solution)/shard_map/ppermute | solution.py:26
  18.4 3.6 %collective-permute-start.1 = (s32[8,128]{1,0:T(8,128)S(1)}, s32[8,128]{1,0:T(8,128)S(1)}, u32[]{:S(2)}, u32[]{:S(2)}) collective-permute-start(s32[8,128]{1,0:T(8,128)S(1)} %add.12.refs_4_), channel_id=1, source_target_pairs={{0,8},{4,12},{8,0},{12,4},{16,24},{20,28},{24,16},{28,20},{1,9},{5... | collective-permute-start | bytes 12296 | tf_op jit(solution)/shard_map/ppermute | solution.py:26
  22.0 1.0 %copy-start.2 = (bf16[128,1024]{1,0:T(8,128)(2,1)S(1)}, bf16[128,1024]{1,0:T(8,128)(2,1)}, u32[]{:S(2)}) copy-start(bf16[128,1024]{1,0:T(8,128)(2,1)} %refs_3_.3) | copy-start | bytes 786436
  23.9 4.8 %copy-start.4 = (bf16[32,1024]{1,0:T(8,128)(2,1)}, bf16[32,1024]{1,0:T(8,128)(2,1)S(1)}, u32[]{:S(2)}) copy-start(bf16[32,1024]{1,0:T(8,128)(2,1)S(1)} %get-tuple-element.35) | copy-start | bytes 196612
  23.9 4.8 %copy-start.5 = (bf16[32,1024]{1,0:T(8,128)(2,1)}, bf16[32,1024]{1,0:T(8,128)(2,1)S(1)}, u32[]{:S(2)}) copy-start(bf16[32,1024]{1,0:T(8,128)(2,1)S(1)} %get-tuple-element.34) | copy-start | bytes 196612
  23.9 4.8 %copy-start.6 = (bf16[32,1024]{1,0:T(8,128)(2,1)}, bf16[32,1024]{1,0:T(8,128)(2,1)S(1)}, u32[]{:S(2)}) copy-start(bf16[32,1024]{1,0:T(8,128)(2,1)S(1)} %get-tuple-element.33) | copy-start | bytes 196612
  23.9 4.8 %copy-start.7 = (bf16[32,1024]{1,0:T(8,128)(2,1)}, bf16[32,1024]{1,0:T(8,128)(2,1)S(1)}, u32[]{:S(2)}) copy-start(bf16[32,1024]{1,0:T(8,128)(2,1)S(1)} %get-tuple-element.31) | copy-start | bytes 196612
  24.0 8.0 %collective-permute-start.5 = (bf16[32,1024]{1,0:T(8,128)(2,1)}, bf16[32,1024]{1,0:T(8,128)(2,1)S(1)}, u32[]{:S(2)}, u32[]{:S(2)}) collective-permute-start(bf16[32,1024]{1,0:T(8,128)(2,1)} %get-tuple-element.28), channel_id=1, source_target_pairs={{0,28},{4,24},{8,20},{12,16},{16,12},{20,8},{24,4},{28,0},{1,29},{... | collective-permute-start | bytes 196616 | tf_op jit(solution)/shard_map/ppermute | solution.py:26
  27.4 6.9 %collective-permute-start.6 = (bf16[32,1024]{1,0:T(8,128)(2,1)}, bf16[32,1024]{1,0:T(8,128)(2,1)S(1)}, u32[]{:S(2)}, u32[]{:S(2)}) collective-permute-start(bf16[32,1024]{1,0:T(8,128)(2,1)} %get-tuple-element.29), channel_id=1, source_target_pairs={{0,24},{4,28},{8,16},{12,20},{16,8},{20,12},{24,0},{28,4},{1,25},{... | collective-permute-start | bytes 196616 | tf_op jit(solution)/shard_map/ppermute | solution.py:26
  28.8 9.0 %collective-permute-start.7 = (bf16[32,1024]{1,0:T(8,128)(2,1)}, bf16[32,1024]{1,0:T(8,128)(2,1)S(1)}, u32[]{:S(2)}, u32[]{:S(2)}) collective-permute-start(bf16[32,1024]{1,0:T(8,128)(2,1)} %get-tuple-element.30), channel_id=1, source_target_pairs={{0,20},{4,16},{8,28},{12,24},{16,4},{20,0},{24,12},{28,8},{1,21},{... | collective-permute-start | bytes 196616 | tf_op jit(solution)/shard_map/ppermute | solution.py:26
  29.6 12.6 %copy-start.3 = (bf16[512,1024]{1,0:T(8,128)(2,1)S(1)}, bf16[512,1024]{1,0:T(8,128)(2,1)}, u32[]{:S(2)}) copy-start(bf16[512,1024]{1,0:T(8,128)(2,1)} %refs_1_.10) | copy-start | bytes 3145732
  29.6 11.1 %collective-permute-start.8 = (bf16[32,1024]{1,0:T(8,128)(2,1)}, bf16[32,1024]{1,0:T(8,128)(2,1)S(1)}, u32[]{:S(2)}, u32[]{:S(2)}) collective-permute-start(bf16[32,1024]{1,0:T(8,128)(2,1)} %copy-done.7), channel_id=1, source_target_pairs={{0,16},{4,20},{8,24},{12,28},{16,0},{20,4},{24,8},{28,12},{1,17},{... | collective-permute-start | bytes 196616 | tf_op jit(solution)/shard_map/ppermute | solution.py:26
  31.9 8.8 %collective-permute-start.9 = (bf16[32,1024]{1,0:T(8,128)(2,1)}, bf16[32,1024]{1,0:T(8,128)(2,1)S(1)}, u32[]{:S(2)}, u32[]{:S(2)}) collective-permute-start(bf16[32,1024]{1,0:T(8,128)(2,1)} %copy-done.6), channel_id=1, source_target_pairs={{0,12},{4,8},{8,4},{12,0},{16,28},{20,24},{24,20},{28,16},{1,13},{... | collective-permute-start | bytes 196616 | tf_op jit(solution)/shard_map/ppermute | solution.py:26
  34.4 6.4 %collective-permute-start.10 = (bf16[32,1024]{1,0:T(8,128)(2,1)}, bf16[32,1024]{1,0:T(8,128)(2,1)S(1)}, u32[]{:S(2)}, u32[]{:S(2)}) collective-permute-start(bf16[32,1024]{1,0:T(8,128)(2,1)} %copy-done.5), channel_id=1, source_target_pairs={{0,8},{4,12},{8,0},{12,4},{16,24},{20,28},{24,16},{28,20},{1,9},{5... | collective-permute-start | bytes 196616 | tf_op jit(solution)/shard_map/ppermute | solution.py:26
  37.7 4.5 %collective-permute-start.11 = (bf16[32,1024]{1,0:T(8,128)(2,1)}, bf16[32,1024]{1,0:T(8,128)(2,1)S(1)}, u32[]{:S(2)}, u32[]{:S(2)}) collective-permute-start(bf16[32,1024]{1,0:T(8,128)(2,1)} %copy-done.4), channel_id=1, source_target_pairs={{0,4},{4,0},{8,12},{12,8},{16,20},{20,16},{24,28},{28,24},{1,5},{5... | collective-permute-start | bytes 196616 | tf_op jit(solution)/shard_map/ppermute | solution.py:26
  40.7 14.6 %collective-permute-start.16 = (bf16[512,1024]{1,0:T(8,128)(2,1)S(1)}, bf16[512,1024]{1,0:T(8,128)(2,1)S(1)}, u32[]{:S(2)}, u32[]{:S(2)}) collective-permute-start(bf16[512,1024]{1,0:T(8,128)(2,1)S(1)} %base_body.5), channel_id=1, source_target_pairs={{0,1},{1,0},{2,3},{3,2},{4,5},{5,4},{6,7},{7,6},{8,9},{9,8},{10,11... | collective-permute-start | bytes 3145736 | tf_op jit(solution)/shard_map/ppermute | solution.py:26
  43.0 3.4 %collective-permute-start.14 = (bf16[32,512]{1,0:T(8,128)(2,1)S(1)}, bf16[32,512]{1,0:T(8,128)(2,1)S(1)}, u32[]{:S(2)}, u32[]{:S(2)}) collective-permute-start(bf16[32,512]{1,0:T(8,128)(2,1)S(1)} %project_body.1.refs_3_), channel_id=1, source_target_pairs={{0,3},{1,2},{2,1},{3,0},{4,7},{5,6},{6,5},{7,4},{8,11},{9,10},{10,... | collective-permute-start | bytes 98312 | tf_op jit(solution)/shard_map/ppermute | solution.py:26
  43.1 4.0 %collective-permute-start.13 = (bf16[32,512]{1,0:T(8,128)(2,1)S(1)}, bf16[32,512]{1,0:T(8,128)(2,1)S(1)}, u32[]{:S(2)}, u32[]{:S(2)}) collective-permute-start(bf16[32,512]{1,0:T(8,128)(2,1)S(1)} %project_body.1.refs_3_), channel_id=1, source_target_pairs={{0,2},{1,3},{2,0},{3,1},{4,6},{5,7},{6,4},{7,5},{8,10},{9,11},{10,... | collective-permute-start | bytes 98312 | tf_op jit(solution)/shard_map/ppermute | solution.py:26
  43.8 3.3 %collective-permute-start.12 = (bf16[32,512]{1,0:T(8,128)(2,1)S(1)}, bf16[32,512]{1,0:T(8,128)(2,1)S(1)}, u32[]{:S(2)}, u32[]{:S(2)}) collective-permute-start(bf16[32,512]{1,0:T(8,128)(2,1)S(1)} %project_body.1.refs_3_), channel_id=1, source_target_pairs={{0,1},{1,0},{2,3},{3,2},{4,5},{5,4},{6,7},{7,6},{8,9},{9,8},{10,11... | collective-permute-start | bytes 98312 | tf_op jit(solution)/shard_map/ppermute | solution.py:26
  47.6 8.5 %collective-permute-start.17 = (bf16[32,1024]{1,0:T(8,128)(2,1)S(1)}, bf16[32,1024]{1,0:T(8,128)(2,1)S(1)}, u32[]{:S(2)}, u32[]{:S(2)}) collective-permute-start(bf16[32,1024]{1,0:T(8,128)(2,1)S(1)} %get-tuple-element.38), channel_id=1, source_target_pairs={{0,28},{4,24},{8,20},{12,16},{16,12},{20,8},{24,4},{28,0},{1,29},{... | collective-permute-start | bytes 196616 | tf_op jit(solution)/shard_map/ppermute | solution.py:26
  50.8 6.9 %collective-permute-start.18 = (bf16[32,1024]{1,0:T(8,128)(2,1)S(1)}, bf16[32,1024]{1,0:T(8,128)(2,1)S(1)}, u32[]{:S(2)}, u32[]{:S(2)}) collective-permute-start(bf16[32,1024]{1,0:T(8,128)(2,1)S(1)} %get-tuple-element.39), channel_id=1, source_target_pairs={{0,24},{4,28},{8,16},{12,20},{16,8},{20,12},{24,0},{28,4},{1,25},{... | collective-permute-start | bytes 196616 | tf_op jit(solution)/shard_map/ppermute | solution.py:26
  51.8 11.6 %collective-permute-start.19 = (bf16[32,1024]{1,0:T(8,128)(2,1)S(1)}, bf16[32,1024]{1,0:T(8,128)(2,1)S(1)}, u32[]{:S(2)}, u32[]{:S(2)}) collective-permute-start(bf16[32,1024]{1,0:T(8,128)(2,1)S(1)} %get-tuple-element.40), channel_id=1, source_target_pairs={{0,20},{4,16},{8,28},{12,24},{16,4},{20,0},{24,12},{28,8},{1,21},{... | collective-permute-start | bytes 196616 | tf_op jit(solution)/shard_map/ppermute | solution.py:26
  51.8 11.6 %collective-permute-start.20 = (bf16[32,1024]{1,0:T(8,128)(2,1)S(1)}, bf16[32,1024]{1,0:T(8,128)(2,1)S(1)}, u32[]{:S(2)}, u32[]{:S(2)}) collective-permute-start(bf16[32,1024]{1,0:T(8,128)(2,1)S(1)} %get-tuple-element.41), channel_id=1, source_target_pairs={{0,16},{4,20},{8,24},{12,28},{16,0},{20,4},{24,8},{28,12},{1,17},{... | collective-permute-start | bytes 196616 | tf_op jit(solution)/shard_map/ppermute | solution.py:26
  55.3 3.5 %copy-start.8 = (bf16[512,1024]{1,0:T(8,128)(2,1)}, bf16[512,1024]{1,0:T(8,128)(2,1)S(1)}, u32[]{:S(2)}) copy-start(bf16[512,1024]{1,0:T(8,128)(2,1)S(1)} %collective-permute-done.16.refs_13_) | copy-start | bytes 3145732
  55.3 8.1 %collective-permute-start.21 = (bf16[32,1024]{1,0:T(8,128)(2,1)S(1)}, bf16[32,1024]{1,0:T(8,128)(2,1)S(1)}, u32[]{:S(2)}, u32[]{:S(2)}) collective-permute-start(bf16[32,1024]{1,0:T(8,128)(2,1)S(1)} %get-tuple-element.43), channel_id=1, source_target_pairs={{0,12},{4,8},{8,4},{12,0},{16,28},{20,24},{24,20},{28,16},{1,13},{... | collective-permute-start | bytes 196616 | tf_op jit(solution)/shard_map/ppermute | solution.py:26
  56.1 7.3 %collective-permute-start.22 = (bf16[32,1024]{1,0:T(8,128)(2,1)S(1)}, bf16[32,1024]{1,0:T(8,128)(2,1)S(1)}, u32[]{:S(2)}, u32[]{:S(2)}) collective-permute-start(bf16[32,1024]{1,0:T(8,128)(2,1)S(1)} %get-tuple-element.44), channel_id=1, source_target_pairs={{0,8},{4,12},{8,0},{12,4},{16,24},{20,28},{24,16},{28,20},{1,9},{5... | collective-permute-start | bytes 196616 | tf_op jit(solution)/shard_map/ppermute | solution.py:26
  57.7 5.8 %collective-permute-start.23 = (bf16[32,1024]{1,0:T(8,128)(2,1)S(1)}, bf16[32,1024]{1,0:T(8,128)(2,1)S(1)}, u32[]{:S(2)}, u32[]{:S(2)}) collective-permute-start(bf16[32,1024]{1,0:T(8,128)(2,1)S(1)} %get-tuple-element.45), channel_id=1, source_target_pairs={{0,4},{4,0},{8,12},{12,8},{16,20},{20,16},{24,28},{28,24},{1,5},{5... | collective-permute-start | bytes 196616 | tf_op jit(solution)/shard_map/ppermute | solution.py:26
